TPU v7x, 32 devices: a whole 2x2x4 slice. The times are simulated.
32 devices in a mesh: batch: 4 (over y, core), space: 8 (over z, x).
Axes of the slice: x: 2, y: 2, z: 4, core: 2. Of those that a mesh axis runs over, the one named last changes fastest.
Arguments:
- features: bfloat16 [3, 32, 8, 16, 1024], P(None, 'batch', 'space'), may hold values from -30 to 30
- view_ids: int32 [3, 32], P(None, 'batch'), may hold values from 0 to 1, as said below
- w_reduce: bfloat16 [1024, 256], replicated, may hold values from -0.1875 to 0.1875
- w_spatial: bfloat16 [2304, 256], replicated, may hold values from -0.125 to 0.125
- w_expand: bfloat16 [256, 1024], replicated, may hold values from -0.375 to 0.375
- w_narrow: bfloat16 [1024, 512], replicated, may hold values from -0.1875 to 0.1875
- w_stride: bfloat16 [4608, 512], replicated, may hold values from -0.09375 to 0.09375
- w_widen: bfloat16 [512, 2048], replicated, may hold values from -0.25 to 0.25
- w_shortcut: bfloat16 [1024, 2048], replicated, may hold values from -0.1875 to 0.1875
- gain_reduce: float32 [256], replicated, may hold values from 0.5 to 1.5
- offset_reduce: float32 [256], replicated, may hold values from -3 to 3
- gain_spatial: float32 [256], replicated, may hold values from 0.5 to 1.5
- offset_spatial: float32 [256], replicated, may hold values from -3 to 3
- gain_expand: float32 [1024], replicated, may hold values from 0.5 to 1.5
- offset_expand: float32 [1024], replicated, may hold values from -3 to 3
- gain_narrow: float32 [512], replicated, may hold values from 0.5 to 1.5
- offset_narrow: float32 [512], replicated, may hold values from -3 to 3
- gain_stride: float32 [512], replicated, may hold values from 0.5 to 1.5
- offset_stride: float32 [512], replicated, may hold values from -3 to 3
- gain_widen: float32 [2048], replicated, may hold values from 0.5 to 1.5
- offset_widen: float32 [2048], replicated, may hold values from -3 to 3
- gain_shortcut: float32 [2048], replicated, may hold values from 0.5 to 1.5
- offset_shortcut: float32 [2048], replicated, may hold values from -3 to 3
- cotangent: bfloat16 [3, 32, 4, 8, 2048], P(None, ('batch', 'space')), may hold values from -6 to 6
Outputs:
- mapped: bfloat16 [3, 32, 4, 8, 2048], P(None, ('batch', 'space'))
- grad_features: bfloat16 [3, 32, 8, 16, 1024], P(None, 'batch', 'space')
- grad_w_reduce: float32 [1024, 256], P('space')
- grad_w_spatial: float32 [2304, 256], P('space')
- grad_w_expand: float32 [256, 1024], P('space')
- grad_w_narrow: float32 [1024, 512], P('space')
- grad_w_stride: float32 [4608, 512], P('space')
- grad_w_widen: float32 [512, 2048], P('space')
- grad_w_shortcut: float32 [1024, 2048], P('space')
- grad_gain_reduce: float32 [256], replicated
- grad_offset_reduce: float32 [256], replicated
- grad_gain_spatial: float32 [256], replicated
- grad_offset_spatial: float32 [256], replicated
- grad_gain_expand: float32 [1024], replicated
- grad_offset_expand: float32 [1024], replicated
- grad_gain_narrow: float32 [512], replicated
- grad_offset_narrow: float32 [512], replicated
- grad_gain_stride: float32 [512], replicated
- grad_offset_stride: float32 [512], replicated
- grad_gain_widen: float32 [2048], replicated
- grad_offset_widen: float32 [2048], replicated
- grad_gain_shortcut: float32 [2048], replicated
- grad_offset_shortcut: float32 [2048], replicated
Inputs may be any that keep to these rules, and one draw needn't show every extreme that they name: `view_ids`: in every micro-batch exactly 16 maps carry each view.
All inputs are finite; a program needn't handle non-finite values.
Results may differ from a plain program's by a relative error of at most 0.025.
Values may be sent and summed in bfloat16 or wider, within the bound.
No kernel may reach another device: no remote copies, remote signals or barrier semaphores. Data moves between devices by JAX's collectives and lax.ppermute only.
A program may use at most 256 MiB of HBM per device.

v0:
```python
import jax
import jax.numpy as jnp
from jax import lax
from jax.sharding import PartitionSpec as P

NVIEW = 2
MICRO = 3


EPSILON = 1e-05
HIGHEST = lax.Precision.HIGHEST


def for_sending(shard):

    def short(part):
        return part.astype(jnp.bfloat16) if part.dtype == jnp.float32 else part

    return jax.tree.map(short, shard)


def gelu_back(value, gradient):
    return jax.vjp(jax.nn.gelu, value)[1](gradient)[0]


def flat_dot(operand, weight):
    layout = operand.shape
    result = jnp.dot(operand.reshape(-1, layout[-1]), weight, preferred_element_type=jnp.float32)
    return result.reshape(layout[:-1] + (weight.shape[1],))


def back_dot(gradient, weight):
    layout = gradient.shape
    result = lax.dot_general(
        gradient.reshape(-1, layout[-1]),
        weight,
        (((1,), (1,)), ((), ())),
        preferred_element_type=jnp.float32,
    )
    return result.reshape(layout[:-1] + (weight.shape[0],))


def weight_grad(operand, gradient):
    return lax.dot_general(
        operand.reshape(-1, operand.shape[-1]),
        gradient.reshape(-1, gradient.shape[-1]),
        (((0,), (0,)), ((), ())),
        preferred_element_type=jnp.float32,
    )


def view_sum(onehot, values):
    return jnp.einsum("mv,mrcn->vn", onehot, values, precision=HIGHEST)


def spread(onehot, per_view):
    return jnp.dot(onehot, per_view, precision=HIGHEST)[:, None, None, :]


def norm_forward(values, onehot, population):
    average = lax.psum(view_sum(onehot, values), ("batch", "space")) / population
    centered = values - spread(onehot, average)
    variance = lax.psum(view_sum(onehot, centered * centered), ("batch", "space")) / population
    inverse = lax.rsqrt(variance + EPSILON)
    return (centered * spread(onehot, inverse), inverse)


def norm_backward(gradient, normed, inverse, onehot, gain, population):
    sum_grad, sum_prod = lax.psum(
        (view_sum(onehot, gradient), view_sum(onehot, gradient * normed)), ("batch", "space")
    )
    result = (
        gain
        * spread(onehot, inverse)
        * (
            gradient
            - spread(onehot, sum_grad) / population
            - normed * spread(onehot, sum_prod) / population
        )
    )
    return (result.astype(jnp.bfloat16), jnp.sum(sum_prod, axis=0), jnp.sum(sum_grad, axis=0))


def pad_columns(values):
    return jnp.pad(values, ((0, 0), (0, 0), (1, 1), (0, 0)))


def pad_forward(values):
    framed = jnp.pad(values, ((0, 0), (1, 1), (0, 0), (0, 0)))
    return pad_columns(framed)


def pad_backward(values):
    framed = jnp.pad(values, ((0, 0), (1, 1), (0, 0), (0, 0)))
    return pad_columns(framed)


def patches(padded, row_count, column_count, step_size):
    pieces = [
        padded[
            :,
            row_step : row_step + row_count : step_size,
            col_step : col_step + column_count : step_size,
        ]
        for row_step in range(3)
        for col_step in range(3)
    ]
    return jnp.concatenate(pieces, axis=-1)


def patches_back(padded, row_count, column_count):
    pieces = [
        padded[
            :, 2 - row_step : 2 - row_step + row_count, 2 - col_step : 2 - col_step + column_count
        ]
        for row_step in range(3)
        for col_step in range(3)
    ]
    return jnp.concatenate(pieces, axis=-1)


def flipped(weight):
    in_width = weight.shape[0] // 9
    out_width = weight.shape[1]
    return (
        weight.reshape(3, 3, in_width, out_width)
        .transpose(0, 1, 3, 2)
        .reshape(9 * out_width, in_width)
    )


def shift_next(piece, axis):
    widths = [(0, 0)] * piece.ndim
    widths[axis] = (0, 1)
    return jnp.pad(lax.slice_in_dim(piece, 1, piece.shape[axis], axis=axis), widths)


def alternate(phases):
    upper = jnp.stack([phases[0][0], phases[0][1]], axis=3)
    lower = jnp.stack([phases[1][0], phases[1][1]], axis=3)
    joined = jnp.stack([upper, lower], axis=2)
    layout = joined.shape
    return joined.reshape(layout[0], layout[1] * 2, layout[3] * 2, layout[5])


def strided_back(gradient, weight):
    in_width = weight.shape[0] // 9
    contrib = back_dot(gradient, weight)
    contrib = contrib.reshape(contrib.shape[:3] + (9, in_width))
    phase_of = (1, 0, 1)
    phases = [[None, None], [None, None]]
    for row_step in range(3):
        for col_step in range(3):
            piece = contrib[:, :, :, row_step * 3 + col_step]
            if row_step == 0:
                piece = shift_next(piece, 1)
            if col_step == 0:
                piece = shift_next(piece, 2)
            row_phase = phase_of[row_step]
            col_phase = phase_of[col_step]
            if phases[row_phase][col_phase] is None:
                phases[row_phase][col_phase] = piece
            else:
                phases[row_phase][col_phase] = phases[row_phase][col_phase] + piece
    return alternate(phases)


def add_even(full, even):
    zero = jnp.zeros_like(even)
    return full + alternate([[even, zero], [zero, zero]])


def on_device(
    features,
    view_ids,
    w_reduce,
    w_spatial,
    w_expand,
    w_narrow,
    w_stride,
    w_widen,
    w_shortcut,
    gain_reduce,
    offset_reduce,
    gain_spatial,
    offset_spatial,
    gain_expand,
    offset_expand,
    gain_narrow,
    offset_narrow,
    gain_stride,
    offset_stride,
    gain_widen,
    offset_widen,
    gain_shortcut,
    offset_shortcut,
    cotangent,
):
    spaces = lax.axis_size("space")
    batches = lax.axis_size("batch")
    local_maps = cotangent.shape[1]
    group_maps = features.shape[1]
    height = features.shape[2] * spaces
    column_count = features.shape[3]
    full_count = group_maps * batches * height * column_count / NVIEW
    half_count = full_count / 4.0
    view_range = jnp.arange(NVIEW)
    first_map = lax.axis_index("space") * local_maps
    weights = (w_reduce, w_spatial, w_expand, w_narrow, w_stride, w_widen, w_shortcut)
    gains = (
        gain_reduce,
        gain_spatial,
        gain_expand,
        gain_narrow,
        gain_stride,
        gain_widen,
        gain_shortcut,
    )
    full_grads = [jnp.zeros(w.shape, jnp.float32) for w in weights]
    share_grads = None
    gain_sums = [jnp.zeros(g.shape, jnp.float32) for g in gains]
    offset_sums = [jnp.zeros(g.shape, jnp.float32) for g in gains]
    outputs = []
    input_grads = []
    for step_index in range(MICRO):
        group_ids = view_ids[step_index]
        own_ids = lax.dynamic_slice_in_dim(group_ids, first_map, local_maps, 0)
        own_hot = (own_ids[:, None] == view_range[None, :]).astype(jnp.float32)
        block_in = lax.all_to_all(
            features[step_index], "space", split_axis=0, concat_axis=1, tiled=True
        )
        row_count = block_in.shape[1]
        pre_reduce = flat_dot(block_in, w_reduce)
        hat_reduce, inv_reduce = norm_forward(pre_reduce, own_hot, full_count)
        act_reduce = gain_reduce * hat_reduce + offset_reduce
        out_reduce = jax.nn.gelu(act_reduce).astype(jnp.bfloat16)
        patch_reduce = patches(pad_forward(out_reduce), row_count, column_count, 1)
        pre_spatial = flat_dot(patch_reduce, w_spatial)
        hat_spatial, inv_spatial = norm_forward(pre_spatial, own_hot, full_count)
        act_spatial = gain_spatial * hat_spatial + offset_spatial
        out_spatial = jax.nn.gelu(act_spatial).astype(jnp.bfloat16)
        pre_expand = flat_dot(out_spatial, w_expand)
        hat_expand, inv_expand = norm_forward(pre_expand, own_hot, full_count)
        residual_one = gain_expand * hat_expand + offset_expand + block_in.astype(jnp.float32)
        joined_rows = jax.nn.gelu(residual_one).astype(jnp.bfloat16)
        pre_narrow = flat_dot(joined_rows, w_narrow)
        hat_narrow, inv_narrow = norm_forward(pre_narrow, own_hot, full_count)
        act_narrow = gain_narrow * hat_narrow + offset_narrow
        out_narrow = jax.nn.gelu(act_narrow).astype(jnp.bfloat16)
        patch_narrow = patches(
            jnp.pad(out_narrow, ((0, 0), (1, 1), (1, 1), (0, 0))), height, column_count, 2
        )
        pre_stride = flat_dot(patch_narrow, w_stride)
        hat_stride, inv_stride = norm_forward(pre_stride, own_hot, half_count)
        act_stride = gain_stride * hat_stride + offset_stride
        out_stride = jax.nn.gelu(act_stride).astype(jnp.bfloat16)
        pre_widen = flat_dot(out_stride, w_widen)
        hat_widen, inv_widen = norm_forward(pre_widen, own_hot, half_count)
        joined_even = joined_rows[:, ::2, ::2]
        pre_shortcut = flat_dot(joined_even, w_shortcut)
        hat_shortcut, inv_shortcut = norm_forward(pre_shortcut, own_hot, half_count)
        residual_two = (
            gain_widen * hat_widen + offset_widen + (gain_shortcut * hat_shortcut + offset_shortcut)
        )
        outputs.append(jax.nn.gelu(residual_two).astype(jnp.bfloat16))
        d_residual_two = gelu_back(residual_two, cotangent[step_index].astype(jnp.float32))
        delta_widen, gain_six, offset_six = norm_backward(
            d_residual_two, hat_widen, inv_widen, own_hot, gain_widen, half_count
        )
        delta_shortcut, gain_seven, offset_seven = norm_backward(
            d_residual_two, hat_shortcut, inv_shortcut, own_hot, gain_shortcut, half_count
        )
        wgrad_widen = weight_grad(out_stride, delta_widen)
        wgrad_shortcut = weight_grad(joined_even, delta_shortcut)
        d_out_stride = back_dot(delta_widen, w_widen)
        delta_stride, gain_five, offset_five = norm_backward(
            gelu_back(act_stride, d_out_stride),
            hat_stride,
            inv_stride,
            own_hot,
            gain_stride,
            half_count,
        )
        wgrad_stride = weight_grad(patch_narrow, delta_stride)
        d_out_narrow = strided_back(delta_stride, w_stride)
        delta_narrow, gain_four, offset_four = norm_backward(
            gelu_back(act_narrow, d_out_narrow),
            hat_narrow,
            inv_narrow,
            own_hot,
            gain_narrow,
            full_count,
        )
        wgrad_narrow = weight_grad(joined_rows, delta_narrow)
        d_joined = add_even(back_dot(delta_narrow, w_narrow), back_dot(delta_shortcut, w_shortcut))
        d_joined = d_joined.astype(jnp.bfloat16)
        d_residual_one = gelu_back(residual_one, d_joined.astype(jnp.float32))
        delta_expand, gain_three, offset_three = norm_backward(
            d_residual_one, hat_expand, inv_expand, own_hot, gain_expand, full_count
        )
        wgrad_expand = weight_grad(out_spatial, delta_expand)
        d_out_spatial = back_dot(delta_expand, w_expand)
        delta_spatial, gain_two, offset_two = norm_backward(
            gelu_back(act_spatial, d_out_spatial),
            hat_spatial,
            inv_spatial,
            own_hot,
            gain_spatial,
            full_count,
        )
        wgrad_spatial = weight_grad(patch_reduce, delta_spatial)
        d_out_reduce = flat_dot(
            patches_back(pad_backward(delta_spatial), row_count, column_count), flipped(w_spatial)
        )
        delta_reduce, gain_one, offset_one = norm_backward(
            gelu_back(act_reduce, d_out_reduce),
            hat_reduce,
            inv_reduce,
            own_hot,
            gain_reduce,
            full_count,
        )
        wgrad_reduce = weight_grad(block_in, delta_reduce)
        d_input = (d_residual_one + back_dot(delta_reduce, w_reduce)).astype(jnp.bfloat16)
        input_grads.append(
            lax.all_to_all(d_input, "space", split_axis=1, concat_axis=0, tiled=True)
        )
        micro_grads = (
            wgrad_reduce,
            wgrad_spatial,
            wgrad_expand,
            wgrad_narrow,
            wgrad_stride,
            wgrad_widen,
            wgrad_shortcut,
        )
        gain_parts = (gain_one, gain_two, gain_three, gain_four, gain_five, gain_six, gain_seven)
        offset_parts = (
            offset_one,
            offset_two,
            offset_three,
            offset_four,
            offset_five,
            offset_six,
            offset_seven,
        )
        gain_sums = [old + new for old, new in zip(gain_sums, gain_parts)]
        offset_sums = [old + new for old, new in zip(offset_sums, offset_parts)]
        full_grads = [old + new for old, new in zip(full_grads, micro_grads)]
    share_grads = list(
        jax.tree.map(
            lambda part: part.astype(jnp.float32),
            lax.psum_scatter(
                for_sending(tuple(full_grads)), "space", scatter_dimension=0, tiled=True
            ),
        )
    )
    weight_totals = jax.tree.map(
        lambda part: part.astype(jnp.float32), lax.psum(for_sending(tuple(share_grads)), "batch")
    )
    norm_outs = []
    for gain_total, offset_total in zip(gain_sums, offset_sums):
        norm_outs.append(gain_total)
        norm_outs.append(offset_total)
    return (jnp.stack(outputs), jnp.stack(input_grads)) + tuple(weight_totals) + tuple(norm_outs)


def solution(mesh):
    return jax.shard_map(
        on_device,
        mesh=mesh,
        in_specs=(
            P(None, "batch", "space", None, None),
            P(None, "batch"),
            P(),
            P(),
            P(),
            P(),
            P(),
            P(),
            P(),
            P(),
            P(),
            P(),
            P(),
            P(),
            P(),
            P(),
            P(),
            P(),
            P(),
            P(),
            P(),
            P(),
            P(),
            P(None, ("batch", "space"), None, None, None),
        ),
        out_specs=(
            P(None, ("batch", "space"), None, None, None),
            P(None, "batch", "space", None, None),
            P("space", None),
            P("space", None),
            P("space", None),
            P("space", None),
            P("space", None),
            P("space", None),
            P("space", None),
            P(),
            P(),
            P(),
            P(),
            P(),
            P(),
            P(),
            P(),
            P(),
            P(),
            P(),
            P(),
            P(),
            P(),
        ),
        check_vma=False,
    )
```

profile of v0, /device:TPU:0, one launch (start us, length us, event | category | flops | bytes accessed | tf_op | source)
XLA Modules:
  0.0 2083.9 jit_solution(16352171523061645244)
XLA Ops:
  9.4 7.3 all-to-all-start.1
  16.6 8.9 all-to-all-done.1
  25.6 3.6 all-to-all-start
  37.7 4.6 all-to-all-start.2
  45.3 5.3 all-to-all-done.2
  53.5 39.1 %all-reduce.56 = (f32[2,256]{1,0:T(2,128)}, f32[2,256]{1,0:T(2,128)}, f32[2,256]{1,0:T(2,128)}) all-reduce(f32[2,256]{1,0:T(2,128)S(1)} %broadcast_multiply_fusion.92, f32[2,256]{1,0:T(2,128)} %broadcast_multiply_fusion.88, f32[2,256]{1,0:T(2,128)} %broadcast_multiply_fusion.84), channel_id=1, replica_groups=mesh['batch'=4,'space'=8] {'batch','space'}, use_global_device_ids=true, to_apply=%region_1.0 | all-reduce | flops 1536 | bytes 12288 | tf_op jit(solution)/shard_map/psum | solution.py:61
  100.9 41.1 %all-reduce.55 = (f32[2,256]{1,0:T(2,128)}, f32[2,256]{1,0:T(2,128)}, f32[2,256]{1,0:T(2,128)}) all-reduce(f32[2,256]{1,0:T(2,128)} %broadcast_multiply_fusion.91, f32[2,256]{1,0:T(2,128)} %broadcast_multiply_fusion.87, f32[2,256]{1,0:T(2,128)} %broadcast_multiply_fusion.83), channel_id=1, replica_groups=mesh['batch'=4,'space'=8] {'batch','space'}, use_global_device_ids=true, to_apply=%region_3.0 | all-reduce | flops 1536 | bytes 12288 | tf_op jit(solution)/shard_map/psum | solution.py:63
  155.9 40.1 %all-reduce.54 = (f32[2,256]{1,0:T(2,128)}, f32[2,256]{1,0:T(2,128)}, f32[2,256]{1,0:T(2,128)}) all-reduce(f32[2,256]{1,0:T(2,128)} %broadcast_multiply_fusion.90, f32[2,256]{1,0:T(2,128)} %broadcast_multiply_fusion.86, f32[2,256]{1,0:T(2,128)S(1)} %broadcast_multiply_fusion.82), channel_id=1, replica_groups=mesh['batch'=4,'space'=8] {'batch','space'}, use_global_device_ids=true, to_apply=%region_5.6 | all-reduce | flops 1536 | bytes 12288 | tf_op jit(solution)/shard_map/psum | solution.py:61
  204.9 41.1 %all-reduce.53 = (f32[2,256]{1,0:T(2,128)}, f32[2,256]{1,0:T(2,128)}, f32[2,256]{1,0:T(2,128)}) all-reduce(f32[2,256]{1,0:T(2,128)} %broadcast_multiply_fusion.89, f32[2,256]{1,0:T(2,128)} %broadcast_multiply_fusion.85, f32[2,256]{1,0:T(2,128)} %broadcast_multiply_fusion.81), channel_id=1, replica_groups=mesh['batch'=4,'space'=8] {'batch','space'}, use_global_device_ids=true, to_apply=%region_7.8 | all-reduce | flops 1536 | bytes 12288 | tf_op jit(solution)/shard_map/psum | solution.py:63
  256.2 40.1 %all-reduce.52 = (f32[2,1024]{1,0:T(2,128)S(1)}, f32[2,1024]{1,0:T(2,128)S(1)}, f32[2,1024]{1,0:T(2,128)S(1)}) all-reduce(f32[2,1024]{1,0:T(2,128)S(1)} %broadcast_multiply_fusion.35, f32[2,1024]{1,0:T(2,128)} %broadcast_multiply_fusion.33, ...), channel_id=1, replica_groups=mesh['batch'=4,'space'=8] {'batch','space'}, use_global_device_ids=true, to_apply=%region_9.10 | all-reduce | flops 6144 | bytes 49152 | tf_op jit(solution)/shard_map/psum | solution.py:61
  302.3 40.9 %all-reduce.51 = (f32[2,1024]{1,0:T(2,128)S(1)}, f32[2,1024]{1,0:T(2,128)S(1)}, f32[2,1024]{1,0:T(2,128)S(1)}) all-reduce(f32[2,1024]{1,0:T(2,128)S(1)} %broadcast_multiply_fusion.34, f32[2,1024]{1,0:T(2,128)S(1)} %broadcast_multiply_fusion.32, ...), channel_id=1, replica_groups=mesh['batch'=4,'space'=8] {'batch','space'}, use_global_device_ids=true, to_apply=%region_11.12 | all-reduce | flops 6144 | bytes 49152 | tf_op jit(solution)/shard_map/psum | solution.py:63
  354.1 39.9 %all-reduce.50 = (f32[2,512]{1,0:T(2,128)}, f32[2,512]{1,0:T(2,128)}, f32[2,512]{1,0:T(2,128)}) all-reduce(f32[2,512]{1,0:T(2,128)} %broadcast_multiply_fusion.62, f32[2,512]{1,0:T(2,128)} %broadcast_multiply_fusion.58, f32[2,512]{1,0:T(2,128)} %broadcast_multiply_fusion.54), channel_id=1, replica_groups=mesh['batch'=4,'space'=8] {'batch','space'}, use_global_device_ids=true, to_apply=%region_13.14 | all-reduce | flops 3072 | bytes 24576 | tf_op jit(solution)/shard_map/psum | solution.py:61
  401.7 41.3 %all-reduce.49 = (f32[2,512]{1,0:T(2,128)}, f32[2,512]{1,0:T(2,128)}, f32[2,512]{1,0:T(2,128)}) all-reduce(f32[2,512]{1,0:T(2,128)} %broadcast_multiply_fusion.61, f32[2,512]{1,0:T(2,128)} %broadcast_multiply_fusion.57, f32[2,512]{1,0:T(2,128)} %broadcast_multiply_fusion.53), channel_id=1, replica_groups=mesh['batch'=4,'space'=8] {'batch','space'}, use_global_device_ids=true, to_apply=%region_15.16 | all-reduce | flops 3072 | bytes 24576 | tf_op jit(solution)/shard_map/psum | solution.py:63
  467.9 2.8 slice.472
  536.4 4.0 fusion.1018
  540.8 3.4 fusion.1019
  545.5 40.1 %all-reduce.48 = (f32[2,512]{1,0:T(2,128)S(1)}, f32[2,512]{1,0:T(2,128)S(1)}, f32[2,512]{1,0:T(2,128)S(1)}) all-reduce(f32[2,512]{1,0:T(2,128)S(1)} %broadcast_multiply_fusion.60, f32[2,512]{1,0:T(2,128)S(1)} %broadcast_multiply_fusion.56, ...), channel_id=1, replica_groups=mesh['batch'=4,'space'=8] {'batch','space'}, use_global_device_ids=true, to_apply=%region_17.18 | all-reduce | flops 3072 | bytes 24576 | tf_op jit(solution)/shard_map/psum | solution.py:61
  588.3 41.0 %all-reduce.47 = (f32[2,512]{1,0:T(2,128)S(1)}, f32[2,512]{1,0:T(2,128)S(1)}, f32[2,512]{1,0:T(2,128)S(1)}) all-reduce(f32[2,512]{1,0:T(2,128)S(1)} %broadcast_multiply_fusion.59, f32[2,512]{1,0:T(2,128)S(1)} %broadcast_multiply_fusion.55, ...), channel_id=1, replica_groups=mesh['batch'=4,'space'=8] {'batch','space'}, use_global_device_ids=true, to_apply=%region_19.20 | all-reduce | flops 3072 | bytes 24576 | tf_op jit(solution)/shard_map/psum | solution.py:63
  643.1 2.9 slice.479
  646.1 2.9 slice.459
  649.0 2.9 slice.439
  651.9 3.9 fusion.1022
  662.4 122.1 %all-reduce.70.cloned.1.call-done = (f32[2,2048]{1,0:T(2,128)}, f32[2,2048]{1,0:T(2,128)}, f32[2,2048]{1,0:T(2,128)}, f32[2,2048]{1,0:T(2,128)}, f32[2,2048]{1,0:T(2,128)}, /*index=5*/f32[2,2048]{1,0:T(2,128)}) async-done(((f32[2,2048]{1,0:T(2,128)}, f32[2,2048]{1,0:T(2,128)}, f32[2,2048]{1,0:T(2,128)}, f32[2,2048]{1,0:T(2,128)}, f32[2,2048]{1,0:T(2,128)}, /*index=5*/f32[2,2048]{1,0:T(2,128)}), ...) | async-done | bytes 98320 | tf_op jit(solution)/shard_map/psum | solution.py:61
  809.7 117.8 %all-reduce.68.cloned.1.call-done = (f32[2,2048]{1,0:T(2,128)}, f32[2,2048]{1,0:T(2,128)}, f32[2,2048]{1,0:T(2,128)}, f32[2,2048]{1,0:T(2,128)}, f32[2,2048]{1,0:T(2,128)}, /*index=5*/f32[2,2048]{1,0:T(2,128)}) async-done(((f32[2,2048]{1,0:T(2,128)}, f32[2,2048]{1,0:T(2,128)}, f32[2,2048]{1,0:T(2,128)}, f32[2,2048]{1,0:T(2,128)}, f32[2,2048]{1,0:T(2,128)}, /*index=5*/f32[2,2048]{1,0:T(2,128)}), ...) | async-done | bytes 98320 | tf_op jit(solution)/shard_map/psum | solution.py:63
  945.3 123.2 %all-reduce.66.cloned.1.call-done = (f32[2,2048]{1,0:T(2,128)}, f32[2,2048]{1,0:T(2,128)}, f32[2,2048]{1,0:T(2,128)}, f32[2,2048]{1,0:T(2,128)}, f32[2,2048]{1,0:T(2,128)}, /*index=5*/f32[2,2048]{1,0:T(2,128)}) async-done(((f32[2,2048]{1,0:T(2,128)}, f32[2,2048]{1,0:T(2,128)}, f32[2,2048]{1,0:T(2,128)}, f32[2,2048]{1,0:T(2,128)}, f32[2,2048]{1,0:T(2,128)}, /*index=5*/f32[2,2048]{1,0:T(2,128)}), ...) | async-done | bytes 98320 | tf_op jit(solution)/shard_map/psum | solution.py:69
  1087.7 42.0 %all-reduce.43 = (f32[2,512]{1,0:T(2,128)S(1)}, f32[2,512]{1,0:T(2,128)S(1)}, f32[2,512]{1,0:T(2,128)S(1)}, f32[2,512]{1,0:T(2,128)S(1)}, f32[2,512]{1,0:T(2,128)S(1)}, /*index=5*/f32[2,512]{1,0:T(2,128)S(1)}) all-reduce(f32[2,512]{1,0:T(2,128)S(1)} %get-tuple-element.467, ...), channel_id=1, replica_groups=mesh['batch'=4,'space'=8] {'batch','space'}, use_global_device_ids=true, to_apply=%region_91.92 | all-reduce | flops 6144 | bytes 49152 | tf_op jit(solution)/shard_map/psum | solution.py:69
  1135.5 3.8 convolution_bitcast_fusion.6
  1141.4 3.8 convolution_bitcast_fusion.7
  1147.2 3.8 convolution_bitcast_fusion.8
  1160.9 121.8 %all-reduce.64.cloned.1.call-done = (f32[2,2048]{1,0:T(2,128)}, f32[2,512]{1,0:T(2,128)}, f32[2,512]{1,0:T(2,128)}, f32[2,2048]{1,0:T(2,128)}, f32[2,512]{1,0:T(...) async-done(((f32[2,2048]{1,0:T(2,128)}, f32[2,512]{1,0:T(2,128)}, f32[2,512]{1,0:T(2,128)}, f32[2,2048]{1,0:T(2,128)}, ...) | async-done | bytes 73744 | tf_op jit(solution)/shard_map/psum | solution.py:69
  1300.7 3.6 fusion.36
  1319.3 3.1 fusion.972
  1328.2 44.9 %all-reduce.41 = (f32[2,1024]{1,0:T(2,128)}, f32[2,1024]{1,0:T(2,128)}, f32[2,1024]{1,0:T(2,128)}, f32[2,1024]{1,0:T(2,128)}, f32[2,1024]{1,0:T(2,128)}, /*index=5*/f32[2,1024]{1,0:T(2,128)}) all-reduce(f32[2,1024]{1,0:T(2,128)} %get-tuple-element.449, ...), channel_id=1, replica_groups=mesh['batch'=4,'space'=8] {'batch','space'}, use_global_device_ids=true, to_apply=%region_101.102 | all-reduce | flops 12288 | bytes 98304 | tf_op jit(solution)/shard_map/psum | solution.py:69
  1387.9 39.4 %all-reduce.40 = (f32[2,256]{1,0:T(2,128)S(1)}, f32[2,256]{1,0:T(2,128)S(1)}, f32[2,256]{1,0:T(2,128)S(1)}, f32[2,256]{1,0:T(2,128)S(1)}, f32[2,256]{1,0:T(2,128)S(1)}, /*index=5*/f32[2,256]{1,0:T(2,128)S(1)}) all-reduce(f32[2,256]{1,0:T(2,128)S(1)} %get-tuple-element.443, ...), channel_id=1, replica_groups=mesh['batch'=4,'space'=8] {'batch','space'}, use_global_device_ids=true, to_apply=%region_105.106 | all-reduce | flops 3072 | bytes 24576 | tf_op jit(solution)/shard_map/psum | solution.py:69
  1441.0 41.1 %all-reduce.39 = (f32[2,256]{1,0:T(2,128)S(1)}, f32[2,256]{1,0:T(2,128)S(1)}, f32[2,256]{1,0:T(2,128)S(1)}, f32[2,256]{1,0:T(2,128)S(1)}, f32[2,256]{1,0:T(2,128)S(1)}, /*index=5*/f32[2,256]{1,0:T(2,128)S(1)}) all-reduce(f32[2,256]{1,0:T(2,128)S(1)} %get-tuple-element.437, ...), channel_id=1, replica_groups=mesh['batch'=4,'space'=8] {'batch','space'}, use_global_device_ids=true, to_apply=%region_109.110 | all-reduce | flops 3072 | bytes 24576 | tf_op jit(solution)/shard_map/psum | solution.py:69
  1513.2 3.5 fusion.1
  1520.6 3.6 fusion
  1542.6 4.5 all-to-all-start.5
  1556.7 6.0 all-to-all-start.4
  1568.3 50.6 %reduce-scatter.12.cloned.1.call-done = bf16[32,1024]{1,0:T(8,128)(2,1)} async-done(((bf16[256,1024]{1,0:T(8,128)(2,1)}), bf16[32,1024]{1,0:T(8,128)(2,1)}) %reduce-scatter.12.cloned.1.call-update) | async-done | bytes 65552 | tf_op jit(solution)/shard_map/reduce_scatter | solution.py:353
  1618.9 66.8 %reduce-scatter.14.cloned.1.call-done = bf16[128,512]{1,0:T(8,128)(2,1)} async-done(((bf16[1024,512]{1,0:T(8,128)(2,1)}), bf16[128,512]{1,0:T(8,128)(2,1)}) %reduce-scatter.14.cloned.1.call-update) | async-done | bytes 131088 | tf_op jit(solution)/shard_map/reduce_scatter | solution.py:353
  1685.7 67.2 %reduce-scatter.10.cloned.1.call-done = bf16[288,256]{1,0:T(8,128)(2,1)} async-done(((bf16[2304,256]{1,0:T(8,128)(2,1)}), bf16[288,256]{1,0:T(8,128)(2,1)}) %reduce-scatter.10.cloned.1.call-update) | async-done | bytes 147472 | tf_op jit(solution)/shard_map/reduce_scatter | solution.py:353
  1752.8 70.2 %reduce-scatter.18.cloned.1.call-done = bf16[64,2048]{1,0:T(8,128)(2,1)} async-done(((bf16[512,2048]{1,0:T(8,128)(2,1)}), bf16[64,2048]{1,0:T(8,128)(2,1)}) %reduce-scatter.18.cloned.1.call-update) | async-done | bytes 262160 | tf_op jit(solution)/shard_map/reduce_scatter | solution.py:353
  1823.1 90.4 %reduce-scatter.20.cloned.1.call-done = bf16[128,2048]{1,0:T(8,128)(2,1)} async-done(((bf16[1024,2048]{1,0:T(8,128)(2,1)}), bf16[128,2048]{1,0:T(8,128)(2,1)}) %reduce-scatter.20.cloned.1.call-update) | async-done | bytes 524304 | tf_op jit(solution)/shard_map/reduce_scatter | solution.py:353
  1913.5 99.3 %reduce-scatter.16.cloned.1.call-done = bf16[576,512]{1,0:T(8,128)(2,1)} async-done(((bf16[4608,512]{1,0:T(8,128)(2,1)}), bf16[576,512]{1,0:T(8,128)(2,1)}) %reduce-scatter.16.cloned.1.call-update) | async-done | bytes 589840 | tf_op jit(solution)/shard_map/reduce_scatter | solution.py:353
  2013.8 4.4 all-to-all-start.3
  2023.7 3.7 all-to-all-done.3
  2029.2 34.5 %all-reduce.72.cloned.1.call-done = (bf16[128,256]{0,1:T(8,128)(2,1)}, bf16[288,256]{1,0:T(8,128)(2,1)}, bf16[32,1024]{1,0:T(8,128)(2,1)}, bf16[128,512]{1,0:T(8...) async-done(((bf16[128,256]{0,1:T(8,128)(2,1)}, bf16[288,256]{1,0:T(8,128)(2,1)}, bf16[32,1024]{1,0:T(8,128)(2,1)}, ...) | async-done | bytes 1785872 | tf_op jit(solution)/shard_map/psum | solution.py:359
  (1294 shorter events, 431.3 us)
Async XLA Ops:
  7.2 624.7 %copy-start = (bf16[512,2048]{1,0:T(8,128)(2,1)S(1)}, bf16[512,2048]{1,0:T(8,128)(2,1)}, u32[]{:S(2)}) copy-start(bf16[512,2048]{1,0:T(8,128)(2,1)} %param.31) | copy-start | bytes 6291460
  9.4 16.2 all-to-all-start.1
  25.5 321.5 %copy-start.29 = (bf16[8,1,16,1024]{3,2,1,0:T(8,128)(2,1)}, bf16[8,1,16,1024]{3,2,1,0:T(8,128)(2,1)S(1)}, u32[]{:S(2)}) copy-start(bf16[8,1,16,1024]{3,2,1,0:T(8,128)(2,1)S(1)} %all-to-all-done.1) | copy-start | bytes 786436
  25.6 12.2 all-to-all-start
  34.9 553.4 %copy-start.151 = (f32[2]{0:T(128)}, f32[2]{0:T(128)S(1)}, u32[]{:S(2)}) copy-start(f32[2]{0:T(128)S(1)} %fusion.798) | copy-start | bytes 28
  35.6 550.9 %copy-start.144 = (f32[2]{0:T(128)}, f32[2]{0:T(128)S(1)}, u32[]{:S(2)}) copy-start(f32[2]{0:T(128)S(1)} %fusion.800) | copy-start | bytes 28
  36.2 551.1 %copy-start.157 = (f32[2]{0:T(128)}, f32[2]{0:T(128)S(1)}, u32[]{:S(2)}) copy-start(f32[2]{0:T(128)S(1)} %fusion.799) | copy-start | bytes 28
  37.7 111.3 %copy-start.32 = (bf16[8,1,16,1024]{3,2,1,0:T(8,128)(2,1)}, bf16[8,1,16,1024]{3,2,1,0:T(8,128)(2,1)S(1)}, u32[]{:S(2)}) copy-start(bf16[8,1,16,1024]{3,2,1,0:T(8,128)(2,1)S(1)} %all-to-all-done) | copy-start | bytes 786436
  37.7 12.8 all-to-all-start.2
  42.3 742.2 %all-reduce.70.cloned.1.call-start = ((), (), s32[]{:S(2)}) async-start(), calls=%async_computation.23 | async-start | bytes 196608 | tf_op jit(solution)/shard_map/psum | solution.py:61
  50.5 100.4 %copy-start.40 = (bf16[8,1,16,1024]{3,2,1,0:T(8,128)(2,1)}, bf16[8,1,16,1024]{3,2,1,0:T(8,128)(2,1)S(1)}, u32[]{:S(2)}) copy-start(bf16[8,1,16,1024]{3,2,1,0:T(8,128)(2,1)S(1)} %all-to-all-done.2) | copy-start | bytes 786436
  50.8 100.3 %copy-start.47 = (f32[128,256]{1,0:T(8,128)}, f32[128,256]{1,0:T(8,128)S(1)}, u32[]{:S(2)}) copy-start(f32[128,256]{1,0:T(8,128)S(1)} %get-tuple-element.488) | copy-start | bytes 393220
  152.0 99.6 %copy-start.6 = (bf16[256,1024]{1,0:T(8,128)(2,1)S(1)}, bf16[256,1024]{1,0:T(8,128)(2,1)}, u32[]{:S(2)}) copy-start(bf16[256,1024]{1,0:T(8,128)(2,1)} %param.28) | copy-start | bytes 1572868
  200.6 95.7 %copy-start.287 = (f32[1,256]{1,0:T(1,128)}, f32[1,256]{1,0:T(1,128)S(1)}, u32[]{:S(2)}) copy-start(f32[1,256]{1,0:T(1,128)S(1)} %fusion.646) | copy-start | bytes 3076
  297.1 343.2 %copy-start.206 = (f32[1,1024]{1,0:T(1,128)}, f32[1,1024]{1,0:T(1,128)S(1)}, u32[]{:S(2)}) copy-start(f32[1,1024]{1,0:T(1,128)S(1)} %fusion.592) | copy-start | bytes 12292
  351.3 151.5 %copy-start.20 = (f32[128,512]{1,0:T(8,128)}, f32[128,512]{1,0:T(8,128)S(1)}, u32[]{:S(2)}) copy-start(f32[128,512]{1,0:T(8,128)S(1)} %get-tuple-element.506) | copy-start | bytes 786436
  352.3 150.5 %copy-start.23 = (f32[128,512]{1,0:T(8,128)}, f32[128,512]{1,0:T(8,128)S(1)}, u32[]{:S(2)}) copy-start(f32[128,512]{1,0:T(8,128)S(1)} %get-tuple-element.504) | copy-start | bytes 786436
  353.4 187.1 %copy-start.26 = (f32[128,512]{1,0:T(8,128)}, f32[128,512]{1,0:T(8,128)S(1)}, u32[]{:S(2)}) copy-start(f32[128,512]{1,0:T(8,128)S(1)} %get-tuple-element.502) | copy-start | bytes 786436
  544.2 87.6 %copy-start.74 = (f32[32,512]{1,0:T(8,128)}, f32[32,512]{1,0:T(8,128)S(1)}, u32[]{:S(2)}) copy-start(f32[32,512]{1,0:T(8,128)S(1)} %get-tuple-element.510) | copy-start | bytes 196612
  545.4 86.4 %copy-start.77 = (f32[32,512]{1,0:T(8,128)}, f32[32,512]{1,0:T(8,128)S(1)}, u32[]{:S(2)}) copy-start(f32[32,512]{1,0:T(8,128)S(1)} %get-tuple-element.512) | copy-start | bytes 196612
  545.5 94.9 %copy-start.8 = (f32[128,1024]{1,0:T(8,128)S(1)}, f32[128,1024]{1,0:T(8,128)}, u32[]{:S(2)}) copy-start(f32[128,1024]{1,0:T(8,128)} %get-tuple-element.500) | copy-start | bytes 1572868
  657.5 279.4 %copy-start.91 = (f32[2048]{0:T(1024)S(1)}, f32[2048]{0:T(1024)}, u32[]{:S(2)}) copy-start(f32[2048]{0:T(1024)} %param.45) | copy-start | bytes 24580
  657.5 279.4 %copy-start.92 = (f32[2048]{0:T(1024)S(1)}, f32[2048]{0:T(1024)}, u32[]{:S(2)}) copy-start(f32[2048]{0:T(1024)} %param.43) | copy-start | bytes 24580
  661.1 266.4 %all-reduce.68.cloned.1.call-start = ((), (), s32[]{:S(2)}) async-start(), calls=%async_computation.22 | async-start | bytes 196608 | tf_op jit(solution)/shard_map/psum | solution.py:63
  803.0 265.5 %all-reduce.66.cloned.1.call-start = ((), (), s32[]{:S(2)}) async-start(), calls=%async_computation.21 | async-start | bytes 196608 | tf_op jit(solution)/shard_map/psum | solution.py:69
  943.9 338.8 %all-reduce.64.cloned.1.call-start = ((), (), s32[]{:S(2)}) async-start(), calls=%async_computation.20 | async-start | bytes 147456 | tf_op jit(solution)/shard_map/psum | solution.py:69
  1151.0 149.7 %copy-start.13 = (f32[32,2048]{1,0:T(8,128)S(1)}, f32[32,2048]{1,0:T(8,128)}, u32[]{:S(2)}) copy-start(f32[32,2048]{1,0:T(8,128)} %get-tuple-element.524) | copy-start | bytes 786436
  1151.1 149.7 %copy-start.53 = (bf16[3,1,4,8,2048]{4,3,2,1,0:T(8,128)(2,1)S(1)}, bf16[3,1,4,8,2048]{4,3,2,1,0:T(8,128)(2,1)}, u32[]{:S(2)}) copy-start(bf16[3,1,4,8,2048]{4,3,2,1,0:T(8,128)(2,1)} %param.47) | copy-start | bytes 1179652
  1151.3 153.1 %copy-start.61 = (f32[1,4,1,8,2,512]{5,3,1,4,2,0:T(8,128)}, f32[1,4,1,8,2,512]{5,3,1,4,2,0:T(8,128)S(1)}, u32[]{:S(2)}) copy-start(f32[1,4,1,8,2,512]{5,3,1,4,2,0:T(8,128)S(1)} %maximum_bitcast_fusion.1) | copy-start | bytes 393220
  1152.8 152.6 %copy-start.17 = (f32[32,2048]{1,0:T(8,128)S(1)}, f32[32,2048]{1,0:T(8,128)}, u32[]{:S(2)}) copy-start(f32[32,2048]{1,0:T(8,128)} %get-tuple-element.518) | copy-start | bytes 786436
  1152.8 152.6 %copy-start.18 = (f32[32,2048]{1,0:T(8,128)S(1)}, f32[32,2048]{1,0:T(8,128)}, u32[]{:S(2)}) copy-start(f32[32,2048]{1,0:T(8,128)} %get-tuple-element.520) | copy-start | bytes 786436
  1159.5 407.2 %reduce-scatter.22.cloned.1.call-start = ((), (), s32[]{:S(2)}) async-start(), calls=%async_computation.19 | async-start | bytes 589824
  1160.9 139.2 %copy-start.202 = (f32[2048]{0:T(1024)}, f32[2048]{0:T(1024)S(1)}, u32[]{:S(2)}) copy-start(f32[2048]{0:T(1024)S(1)} %get-tuple-element.370) | copy-start | bytes 24580
  1492.3 126.6 %reduce-scatter.12.cloned.1.call-start = ((), (), s32[]{:S(2)}) async-start(), calls=%async_computation.14 | async-start | bytes 589824 | tf_op jit(solution)/shard_map/reduce_scatter | solution.py:353
  1498.9 186.8 %reduce-scatter.14.cloned.1.call-start = ((), (), s32[]{:S(2)}) async-start(), calls=%async_computation.15 | async-start | bytes 1179648 | tf_op jit(solution)/shard_map/reduce_scatter | solution.py:353
  1501.8 251.0 %reduce-scatter.10.cloned.1.call-start = ((), (), s32[]{:S(2)}) async-start(), calls=%async_computation.13 | async-start | bytes 1327104 | tf_op jit(solution)/shard_map/reduce_scatter | solution.py:353
  1505.3 317.8 %reduce-scatter.18.cloned.1.call-start = ((), (), s32[]{:S(2)}) async-start(), calls=%async_computation.17 | async-start | bytes 2359296 | tf_op jit(solution)/shard_map/reduce_scatter | solution.py:353
  1510.3 403.2 %reduce-scatter.20.cloned.1.call-start = ((), (), s32[]{:S(2)}) async-start(), calls=%async_computation.18 | async-start | bytes 4718592 | tf_op jit(solution)/shard_map/reduce_scatter | solution.py:353
  1516.7 496.0 %reduce-scatter.16.cloned.1.call-start = ((), (), s32[]{:S(2)}) async-start(), calls=%async_computation.16 | async-start | bytes 5308416 | tf_op jit(solution)/shard_map/reduce_scatter | solution.py:353
  1525.1 487.7 %copy-start.98 = (bf16[128,256]{1,0:T(8,128)(2,1)S(1)}, bf16[128,256]{1,0:T(8,128)(2,1)}, u32[]{:S(2)}) copy-start(bf16[128,256]{1,0:T(8,128)(2,1)} %copy-done.97) | copy-start | bytes 196612
  1526.2 486.6 %copy-start.55 = (f32[8,16,1024]{2,1,0:T(8,128)S(1)}, f32[8,16,1024]{2,1,0:T(8,128)}, u32[]{:S(2)}) copy-start(f32[8,16,1024]{2,1,0:T(8,128)} %get-tuple-element.528) | copy-start | bytes 1572868
  1527.0 495.4 %copy-start.325 = (f32[2,1024]{1,0:T(2,128)S(1)}, f32[2,1024]{1,0:T(2,128)}, u32[]{:S(2)}) copy-start(f32[2,1024]{1,0:T(2,128)} %get-tuple-element.194) | copy-start | bytes 24580
  1535.7 540.5 %copy-start.250 = (f32[2048]{0:T(1024)}, f32[2048]{0:T(1024)S(1)}, u32[]{:S(2)}) copy-start(f32[2048]{0:T(1024)S(1)} %add_add_fusion.4) | copy-start | bytes 24580
  1542.6 14.0 all-to-all-start.5
  1556.7 457.2 %all-to-all-start.4 = ((bf16[1,8,16,1024]{3,2,0,1:T(8,128)(2,1)}), bf16[1,8,16,1024]{3,2,0,1:T(8,128)(2,1)}, u32[]{:S(2)}, u32[]{:S(2)}) async-start(bf16[1,8,16,1024]{3,2,0,1:T(8,128)(2,1)} %fusion.28), calls=%async_computation.4 | async-start | bytes 524288 | tf_op jit(solution)/shard_map/all_to_all | solution.py:326
  1562.7 501.1 %all-reduce.72.cloned.1.call-start = ((), (), s32[]{:S(2)}) async-start(), calls=%async_computation.24 | async-start | bytes 3571712 | tf_op jit(solution)/shard_map/psum | solution.py:359
  2012.8 64.0 %copy-start.1 = (bf16[512,2048]{1,0:T(8,128)(2,1)S(1)}, bf16[512,2048]{1,0:T(8,128)(2,1)}, u32[]{:S(2)}) copy-start(bf16[512,2048]{1,0:T(8,128)(2,1)} %param.31) | copy-start | bytes 6291460
  2013.8 13.5 all-to-all-start.3
  (332 other events, 3004.6 us)
Sparse Core Ops, SparseCore 0:
  661.2 123.2 all-reduce.69
  803.1 124.4 all-reduce.67
  944.0 124.4 all-reduce.65
  1159.7 123.0 all-reduce.63
  1492.4 62.0 reduce-scatter.21
  1557.7 61.1 reduce-scatter.11
  1623.2 62.3 reduce-scatter.13
  1689.6 63.1 reduce-scatter.9
  1756.4 66.6 reduce-scatter.17
  1826.6 86.8 reduce-scatter.19
  1917.5 95.1 reduce-scatter.15
  2016.4 47.3 all-reduce.71
where the time goes:
time: 2110 us; the launch traced here: 2080 us
  waiting for transfers between devices  983 us (47%)
  blocking collectives  572 us (27%)
  matrix products  201 us (10%)
  local copies, waits for them, and re-layouts  139 us (7%)
  other arithmetic  137 us (6%)
  starting transfers between devices  31.3 us (1%)
    reduce_scatter x6, waiting for transfers between devices, on_device(): lax.psum_scatter(for_sending(tuple(full_grads)), 'space', scatter_dimensi...  444 us
    psum x2, waiting for transfers between devices, norm_backward(): lax.psum((view_sum(onehot, gradient), view_sum(onehot, gradient * normed)...  245 us
    psum x5, blocking collectives, norm_forward(): lax.psum(view_sum(onehot, centered * centered), ('batch', 'space'))  205 us
    psum x5, blocking collectives, norm_forward(): lax.psum(view_sum(onehot, values), ('batch', 'space')) / population  199 us
    psum x4, blocking collectives, norm_backward(): lax.psum((view_sum(onehot, gradient), view_sum(onehot, gradient * normed)...  167 us
    psum x1, waiting for transfers between devices, norm_forward(): lax.psum(view_sum(onehot, values), ('batch', 'space')) / population  122 us
    psum x1, waiting for transfers between devices, norm_forward(): lax.psum(view_sum(onehot, centered * centered), ('batch', 'space'))  118 us
    dot_general x81, matrix products, spread(): return jnp.dot(onehot, per_view, precision=HIGHEST)[:, None, None, :]  103 us
  transfers between devices with their start and end apart: 18, of which 15 were waited for; matrix products, arithmetic and copies ran while one was open for 4% of the time, Pallas kernels for 0%

commit v1 on v0

v1 whole, which is shorter than its diff:
```python
import jax
import jax.numpy as jnp
from jax import lax
from jax.sharding import PartitionSpec as P

NVIEW = 2
MICRO = 3
EPSILON = 1e-05
BF = jnp.bfloat16
F32 = jnp.float32
ALL = ("batch", "space")


def dot(a, b, dims=((1,), (0,))):
    return lax.dot_general(a, b, (dims, ((), ())), preferred_element_type=F32)


def dot_nt(a, b):
    return dot(a, b, ((1,), (1,)))


def dot_tn(a, b):
    return dot(a, b, ((0,), (0,)))


def gelu_back(value, gradient):
    return jax.vjp(jax.nn.gelu, value)[1](gradient)[0]


def share(block, count):
    copies = jnp.broadcast_to(block[None], (count,) + block.shape)
    return lax.all_to_all(copies, ALL, 0, 0, tiled=True)


def spread_slots(parts, count):
    return lax.all_to_all(parts, ALL, 0, 0, tiled=True)


def local_stats(values):
    mean = jnp.mean(values, axis=1)
    square = jnp.sum((values - mean[:, None, :]) ** 2, axis=1)
    return jnp.stack([mean, square], axis=1)


def merge_stats(gathered, weight, rows):
    count = jnp.sum(weight, axis=0)[:, None]
    means, squares = gathered[:, :, 0], gathered[:, :, 1]
    wide = weight[:, :, None]
    mean = jnp.sum(wide * means, axis=0) / count
    total = jnp.sum(wide * (squares + rows * (means - mean[None]) ** 2), axis=0)
    return mean, lax.rsqrt(total / (count * rows) + EPSILON)


def shift_rows(values, axis, offset):
    if offset == 0:
        return values
    size = values.shape[axis]
    widths = [(0, 0)] * values.ndim
    if offset > 0:
        widths[axis] = (0, offset)
        return jnp.pad(lax.slice_in_dim(values, offset, size, axis=axis), widths)
    widths[axis] = (-offset, 0)
    return jnp.pad(lax.slice_in_dim(values, 0, size + offset, axis=axis), widths)


def neighbour(maps, phase_y, phase_x, step_y, step_x):
    at_y, at_x = phase_y + step_y, phase_x + step_x
    piece = maps[:, at_y % 2, at_x % 2]
    return shift_rows(shift_rows(piece, 1, at_y // 2), 2, at_x // 2)


def patches(maps, sign):
    return jnp.stack(
        [
            jnp.stack(
                [
                    jnp.concatenate(
                        [neighbour(maps, py, px, sign * (r - 1), sign * (c - 1)) for r in range(3) for c in range(3)],
                        axis=-1,
                    )
                    for px in range(2)
                ],
                axis=1,
            )
            for py in range(2)
        ],
        axis=1,
    )


def on_device(
    features,
    view_ids,
    w_reduce,
    w_spatial,
    w_expand,
    w_narrow,
    w_stride,
    w_widen,
    w_shortcut,
    gain_reduce,
    offset_reduce,
    gain_spatial,
    offset_spatial,
    gain_expand,
    offset_expand,
    gain_narrow,
    offset_narrow,
    gain_stride,
    offset_stride,
    gain_widen,
    offset_widen,
    gain_shortcut,
    offset_shortcut,
    cotangent,
):
    ns = lax.axis_size("space")
    nb = lax.axis_size("batch")
    n = ns * nb
    maps = features.shape[1]
    cols = features.shape[3]
    xh = cols // 2
    yh = ns // 2
    rows = ns * cols
    half = rows // 4
    c_in = features.shape[4]
    c_mid = w_reduce.shape[1]
    assert features.shape[2] == 1 and cotangent.shape[1] == 1 and maps == ns

    def to_maps(block):
        c = block.shape[-1]
        return block.reshape(yh, 2, MICRO, 2, xh, c).transpose(2, 1, 3, 0, 4, 5)

    def to_rows(block):
        c = block.shape[-1]
        return block.reshape(MICRO, 2, 2, yh, xh, c).transpose(3, 1, 0, 2, 4, 5).reshape(ns, MICRO, cols, c)

    def exchange(block):
        return lax.all_to_all(block, "space", 0, 0, tiled=True)

    rows_in = features.reshape(MICRO, maps, xh, 2, c_in).transpose(1, 0, 3, 2, 4).reshape(maps, MICRO, cols, c_in)
    pre_rows = dot(rows_in.reshape(-1, c_in), w_reduce).reshape(maps, MICRO, cols, c_mid)

    ids = view_ids.T.astype(F32)
    hot = jnp.stack([(ids == v).astype(F32) for v in range(NVIEW)], axis=-1)
    count_here = jnp.sum(hot, axis=0) * cols
    sum_here = jnp.einsum("kmv,kmpc->mvc", hot, pre_rows, precision=lax.Precision.HIGHEST)
    mean_here = sum_here / jnp.maximum(count_here, 1.0)[:, :, None]
    own_mean = jnp.einsum("kmv,mvc->kmc", hot, mean_here, precision=lax.Precision.HIGHEST)
    square_here = jnp.einsum(
        "kmv,kmpc->mvc", hot, (pre_rows - own_mean[:, :, None, :]) ** 2, precision=lax.Precision.HIGHEST
    )
    payload = jnp.concatenate(
        [
            mean_here.reshape(MICRO * NVIEW, c_mid),
            square_here.reshape(MICRO * NVIEW, c_mid),
            jnp.broadcast_to(count_here.reshape(MICRO * NVIEW, 1), (MICRO * NVIEW, c_mid)),
            jnp.pad(ids.reshape(1, -1), ((0, 0), (0, c_mid - ids.size))),
        ],
        axis=0,
    )
    got = share(payload, n)
    k = MICRO * NVIEW
    g_mean, g_square, g_count = got[:, :k], got[:, k : 2 * k], got[:, 2 * k : 3 * k]
    population = jnp.sum(g_count, axis=0)
    mean_views = jnp.sum(g_count * g_mean, axis=0) / population
    var_views = jnp.sum(g_square + g_count * (g_mean - mean_views) ** 2, axis=0) / population
    inv_views = lax.rsqrt(var_views + EPSILON)
    mean_views = mean_views.reshape(MICRO, NVIEW, c_mid)
    inv_views = inv_views.reshape(MICRO, NVIEW, c_mid)

    all_ids = got[:, 3 * k, : ids.size].reshape(nb, ns, maps, MICRO)[:, 0].reshape(n, MICRO)
    me = lax.axis_index("batch") * ns + lax.axis_index("space")
    my_ids = lax.dynamic_slice_in_dim(all_ids, me, 1, 0)
    weight = (all_ids == my_ids).astype(F32)
    mates = jnp.sum(weight, axis=0)[:, None]
    my_view = my_ids[0][:, None]

    def pick(per_view):
        return jnp.where(my_view > 0.5, per_view[:, 1], per_view[:, 0])

    def stats_of(values):
        m, r, c = values.shape
        return merge_stats(share(local_stats(values), n), weight, r)

    def sums_of(gradient, hat):
        block = jnp.stack([jnp.sum(gradient, axis=1), jnp.sum(gradient * hat, axis=1)], axis=1)
        got = share(block, n)
        return jnp.sum(weight[:, :, None, None] * got, axis=0), jnp.sum(got, axis=(0, 1)), got

    def norm_back(gradient, hat, inverse, gain, sums, size):
        count = mates * size
        return (
            (gain * inverse)[:, None, :]
            * (gradient - (sums[:, 0] / count)[:, None, :] - hat * (sums[:, 1] / count)[:, None, :])
        ).astype(BF)

    maps_in = to_maps(exchange(rows_in)).reshape(MICRO, rows, c_in)
    pre_reduce = to_maps(exchange(pre_rows)).reshape(MICRO, rows, c_mid)
    mean_reduce, inv_reduce = pick(mean_views), pick(inv_views)
    hat_reduce = (pre_reduce - mean_reduce[:, None]) * inv_reduce[:, None]
    act_reduce = gain_reduce * hat_reduce + offset_reduce
    out_reduce = jax.nn.gelu(act_reduce).astype(BF)

    grid = (MICRO, 2, 2, yh, xh)
    patch_reduce = patches(out_reduce.reshape(grid + (c_mid,)), 1).reshape(MICRO * rows, 9 * c_mid)
    pre_spatial = dot(patch_reduce, w_spatial).reshape(MICRO, rows, c_mid)
    mean, inv_spatial = stats_of(pre_spatial)
    hat_spatial = (pre_spatial - mean[:, None]) * inv_spatial[:, None]
    act_spatial = gain_spatial * hat_spatial + offset_spatial
    out_spatial = jax.nn.gelu(act_spatial).astype(BF)

    pre_expand = dot(out_spatial.reshape(-1, c_mid), w_expand).reshape(MICRO, rows, c_in)
    mean, inv_expand = stats_of(pre_expand)
    hat_expand = (pre_expand - mean[:, None]) * inv_expand[:, None]
    residual_one = gain_expand * hat_expand + offset_expand + maps_in.astype(F32)
    joined = jax.nn.gelu(residual_one).astype(BF)

    c_wide = w_narrow.shape[1]
    pre_narrow = dot(joined.reshape(-1, c_in), w_narrow).reshape(MICRO, rows, c_wide)
    joined_even = joined[:, :half].reshape(-1, c_in)
    mean, inv_narrow = stats_of(pre_narrow)
    hat_narrow = (pre_narrow - mean[:, None]) * inv_narrow[:, None]
    act_narrow = gain_narrow * hat_narrow + offset_narrow
    out_narrow = jax.nn.gelu(act_narrow).astype(BF)

    narrow_maps = out_narrow.reshape(grid + (c_wide,))
    patch_narrow = jnp.concatenate(
        [neighbour(narrow_maps, 0, 0, r - 1, c - 1) for r in range(3) for c in range(3)], axis=-1
    ).reshape(MICRO * half, 9 * c_wide)
    pre_stride = dot(patch_narrow, w_stride).reshape(MICRO, half, c_wide)
    mean, inv_stride = stats_of(pre_stride)
    hat_stride = (pre_stride - mean[:, None]) * inv_stride[:, None]
    act_stride = gain_stride * hat_stride + offset_stride
    out_stride = jax.nn.gelu(act_stride).astype(BF).reshape(-1, c_wide)

    c_out = w_widen.shape[1]
    pre_widen = dot(out_stride, w_widen).reshape(MICRO, half, c_out)
    pre_shortcut = dot(joined_even, w_shortcut).reshape(MICRO, half, c_out)
    both = jnp.concatenate([local_stats(pre_widen), local_stats(pre_shortcut)], axis=-1)
    width = 2 * c_out // n
    pieces = spread_slots(both.reshape(MICRO * 2, n, width).transpose(1, 0, 2), n)
    pieces = pieces.reshape(n, MICRO, 2, width)
    view_results = []
    for view in range(NVIEW):
        mean, inverse = merge_stats(pieces, (all_ids == view).astype(F32), half)
        view_results.append(jnp.stack([mean, inverse], axis=1))
    whole = share(jnp.stack(view_results, axis=1), n)
    whole = whole.transpose(1, 2, 3, 0, 4).reshape(MICRO, NVIEW, 2, 2 * c_out)
    whole = pick(whole.reshape(MICRO, NVIEW, 4 * c_out)).reshape(MICRO, 2, 2, c_out)
    mean_widen, mean_shortcut = whole[:, 0, 0], whole[:, 0, 1]
    inv_widen, inv_shortcut = whole[:, 1, 0], whole[:, 1, 1]
    hat_widen = (pre_widen - mean_widen[:, None]) * inv_widen[:, None]
    hat_shortcut = (pre_shortcut - mean_shortcut[:, None]) * inv_shortcut[:, None]
    residual_two = gain_widen * hat_widen + offset_widen + (gain_shortcut * hat_shortcut + offset_shortcut)
    mapped = jax.nn.gelu(residual_two).astype(BF).reshape(cotangent.shape)
    d_two = gelu_back(residual_two, cotangent.reshape(MICRO, half, c_out).astype(F32))

    block = jnp.stack(
        [jnp.sum(d_two, axis=1), jnp.sum(d_two * hat_widen, axis=1), jnp.sum(d_two * hat_shortcut, axis=1)], axis=1
    )
    width = c_out // n
    pieces = spread_slots(block.reshape(MICRO * 3, n, width).transpose(1, 0, 2), n).reshape(n, MICRO, 3, width)
    by_view = jnp.stack(
        [jnp.sum((all_ids == view).astype(F32)[:, :, None, None] * pieces, axis=0) for view in range(NVIEW)], axis=1
    )
    whole = share(by_view, n).transpose(1, 2, 3, 0, 4).reshape(MICRO, NVIEW, 3, c_out)
    totals = jnp.sum(whole, axis=(0, 1))
    grad_offset_widen, grad_gain_widen, grad_gain_shortcut = totals[0], totals[1], totals[2]
    sums = pick(whole.reshape(MICRO, NVIEW, 3 * c_out)).reshape(MICRO, 3, c_out)
    delta_widen = norm_back(d_two, hat_widen, inv_widen, gain_widen, sums[:, :2], half).reshape(-1, c_out)
    delta_shortcut = norm_back(d_two, hat_shortcut, inv_shortcut, gain_shortcut, sums[:, ::2], half).reshape(-1, c_out)

    def gathered_grad(operand, gradient):
        share_cols = gradient.shape[1] // nb
        parts = gradient.reshape(-1, nb, share_cols).transpose(1, 0, 2)
        parts = lax.all_to_all(parts, "batch", 0, 0, tiled=True).reshape(-1, share_cols)
        copies = jnp.broadcast_to(operand[None], (nb,) + operand.shape)
        copies = lax.all_to_all(copies, "batch", 0, 0, tiled=True).reshape(-1, operand.shape[1])
        return dot_tn(copies, parts).astype(BF)

    def finish_cols(product):
        r, c = product.shape
        mine = lax.all_to_all(product.reshape(ns, r // ns, c), "space", 0, 0, tiled=True)
        mine = jnp.sum(mine.astype(F32), axis=0).astype(BF)
        return lax.all_gather(mine, "batch", axis=1, tiled=True).astype(F32)

    def finish_rows(product):
        r, c = product.shape
        parts = product.astype(BF).reshape(ns, nb, r // n, c)
        parts = lax.all_to_all(parts, "batch", 1, 1, tiled=True)
        parts = jnp.sum(parts.astype(F32), axis=1).astype(BF)
        mine = lax.all_to_all(parts, "space", 0, 0, tiled=True)
        mine = jnp.sum(mine.astype(F32), axis=0).astype(BF)
        return lax.all_gather(mine, "batch", axis=0, tiled=True).astype(F32)

    grad_w_widen = finish_cols(gathered_grad(out_stride, delta_widen))
    grad_w_shortcut = finish_cols(gathered_grad(joined_even, delta_shortcut))

    d_out_stride = dot_nt(delta_widen, w_widen).reshape(MICRO, half, c_wide)
    d_stride = gelu_back(act_stride, d_out_stride)
    sums, totals, _ = sums_of(d_stride, hat_stride)
    grad_offset_stride, grad_gain_stride = totals[0], totals[1]
    delta_stride = norm_back(d_stride, hat_stride, inv_stride, gain_stride, sums, half).reshape(-1, c_wide)
    grad_w_stride = finish_rows(dot_tn(patch_narrow, delta_stride))

    contrib = dot_nt(delta_stride, w_stride).reshape(MICRO, yh, xh, 9, c_wide)
    phases = [[None, None], [None, None]]
    for r in range(3):
        for c in range(3):
            piece = contrib[:, :, :, r * 3 + c]
            piece = shift_rows(shift_rows(piece, 1, 1 if r == 0 else 0), 2, 1 if c == 0 else 0)
            old = phases[(r + 1) % 2][(c + 1) % 2]
            phases[(r + 1) % 2][(c + 1) % 2] = piece if old is None else old + piece
    d_out_narrow = jnp.stack([jnp.stack(line, axis=1) for line in phases], axis=1).reshape(MICRO, rows, c_wide)
    d_narrow = gelu_back(act_narrow, d_out_narrow)
    sums, totals, _ = sums_of(d_narrow, hat_narrow)
    grad_offset_narrow, grad_gain_narrow = totals[0], totals[1]
    delta_narrow = norm_back(d_narrow, hat_narrow, inv_narrow, gain_narrow, sums, rows).reshape(-1, c_wide)
    grad_w_narrow = finish_rows(dot_tn(joined.reshape(-1, c_in), delta_narrow))

    d_joined = dot_nt(delta_narrow, w_narrow).reshape(MICRO, rows, c_in)
    d_even = dot_nt(delta_shortcut, w_shortcut).reshape(MICRO, half, c_in)
    d_joined = jnp.concatenate([d_joined[:, :half] + d_even, d_joined[:, half:]], axis=1).astype(BF)
    d_one = gelu_back(residual_one, d_joined.astype(F32))
    d_one_rows = exchange(to_rows(d_one.astype(BF)))
    sums, totals, _ = sums_of(d_one, hat_expand)
    grad_offset_expand, grad_gain_expand = totals[0], totals[1]
    delta_expand = norm_back(d_one, hat_expand, inv_expand, gain_expand, sums, rows).reshape(-1, c_in)
    grad_w_expand = finish_rows(dot_tn(out_spatial.reshape(-1, c_mid), delta_expand))

    d_out_spatial = dot_nt(delta_expand, w_expand).reshape(MICRO, rows, c_mid)
    d_spatial = gelu_back(act_spatial, d_out_spatial)
    sums, totals, _ = sums_of(d_spatial, hat_spatial)
    grad_offset_spatial, grad_gain_spatial = totals[0], totals[1]
    delta_spatial = norm_back(d_spatial, hat_spatial, inv_spatial, gain_spatial, sums, rows).reshape(-1, c_mid)
    grad_w_spatial = finish_rows(dot_tn(patch_reduce, delta_spatial))

    patch_delta = patches(delta_spatial.reshape(grid + (c_mid,)), -1).reshape(MICRO * rows, 9 * c_mid)
    flipped = w_spatial.reshape(9, c_mid, c_mid).transpose(0, 2, 1).reshape(9 * c_mid, c_mid)
    d_out_reduce = dot(patch_delta, flipped).reshape(MICRO, rows, c_mid)
    d_reduce = gelu_back(act_reduce, d_out_reduce)
    d_rows = exchange(to_rows(d_reduce))
    _, totals, got = sums_of(d_reduce, hat_reduce)
    grad_offset_reduce, grad_gain_reduce = totals[0], totals[1]
    view_sums = jnp.stack(
        [jnp.sum((all_ids == view).astype(F32)[:, :, None, None] * got, axis=0) for view in range(NVIEW)], axis=1
    )
    counts = population.reshape(MICRO, NVIEW, c_mid)

    def at_rows(per_view):
        chosen = jnp.where(ids[:, :, None] > 0.5, per_view[None, :, 1], per_view[None, :, 0])
        return chosen[:, :, None, :]

    hat_rows = (pre_rows - at_rows(mean_views)) * at_rows(inv_views)
    delta_reduce = (
        gain_reduce
        * at_rows(inv_views)
        * (d_rows - at_rows(view_sums[:, :, 0] / counts) - hat_rows * at_rows(view_sums[:, :, 1] / counts))
    ).astype(BF).reshape(-1, c_mid)
    grad_w_reduce = finish_rows(dot_tn(rows_in.reshape(-1, c_in), delta_reduce))
    d_input = (d_one_rows.reshape(-1, c_in).astype(F32) + dot_nt(delta_reduce, w_reduce)).astype(BF)
    grad_features = (
        d_input.reshape(maps, MICRO, 2, xh, c_in).transpose(1, 0, 3, 2, 4).reshape(features.shape)
    )

    return (
        mapped,
        grad_features,
        grad_w_reduce,
        grad_w_spatial,
        grad_w_expand,
        grad_w_narrow,
        grad_w_stride,
        grad_w_widen,
        grad_w_shortcut,
        grad_gain_reduce,
        grad_offset_reduce,
        grad_gain_spatial,
        grad_offset_spatial,
        grad_gain_expand,
        grad_offset_expand,
        grad_gain_narrow,
        grad_offset_narrow,
        grad_gain_stride,
        grad_offset_stride,
        grad_gain_widen,
        grad_offset_widen,
        grad_gain_shortcut,
        grad_offset_widen,
    )


def solution(mesh):
    return jax.shard_map(
        on_device,
        mesh=mesh,
        in_specs=(P(None, "batch", "space", None, None), P(None, "batch"))
        + (P(),) * 21
        + (P(None, ("batch", "space"), None, None, None),),
        out_specs=(P(None, ("batch", "space"), None, None, None), P(None, "batch", "space", None, None))
        + (P("space", None),) * 7
        + (P(),) * 14,
        check_vma=False,
    )
```

time: 2110 us -> 764 us (0.36)
  waiting for transfers between devices: 983 us -> 333 us
  blocking collectives: 572 us -> 58 us
  matrix products: 201 us -> 35.4 us
  starting transfers between devices: 31.3 us -> 122 us
  other arithmetic: 137 us -> 82.9 us
  local copies, waits for them, and re-layouts: 139 us -> 115 us
    psum x14 -> x0, blocking collectives: 572 us -> none  [the longest x5 205 us: norm_forward(): lax.psum(view_sum(onehot, centered * centered), ('batch', 'space'))]
    psum x5 -> x0, waiting for transfers between devices: 519 us -> none  [the longest x2 245 us: norm_backward(): lax.psum((view_sum(onehot, gradient), view_sum(onehot, gradient * normed)...]
    reduce_scatter x6 -> x0, waiting for transfers between devices: 444 us -> none  [on_device(): lax.psum_scatter(for_sending(tuple(full_grads)), 'space', scatter_dimensi...]
    all_to_all x6 -> x33, waiting for transfers between devices: 19.3 us -> 333 us  [the longest x11 110 us: share(): return lax.all_to_all(copies, ALL, 0, 0, tiled=True)]
    dot_general x144 -> x24, matrix products: 201 us -> 35.4 us  [the longest x21 34.9 us: dot(): return lax.dot_general(a, b, (dims, ((), ())), preferred_element_type=F32)]
    all_to_all x6 -> x33, starting transfers between devices: 30.3 us -> 122 us  [the longest x11 38.6 us: share(): return lax.all_to_all(copies, ALL, 0, 0, tiled=True)]
    slice x57 -> x52, local copies, waits for them, and re-layouts: 84.7 us -> 13.1 us  [the longest x2 4.38 us: pick(): return jnp.where(my_view > 0.5, per_view[:, 1], per_view[:, 0])]
    all_gather x0 -> x7, blocking collectives: none -> 42.4 us  [the longest x5 29.2 us: finish_rows(): return lax.all_gather(mine, 'batch', axis=0, tiled=True).astype(F32)]
  transfers between devices with their start and end apart: 18 -> 33, of which waited for: 15 -> 32; matrix products, arithmetic and copies ran while one was open for 4% -> 15% of each run, Pallas kernels for 0% -> 0%
where the time goes in v1:
time: 764 us; the launch traced here: 751 us
  waiting for transfers between devices  333 us (44%)
  starting transfers between devices  122 us (16%)
  local copies, waits for them, and re-layouts  115 us (15%)
  other arithmetic  82.9 us (11%)
  blocking collectives  58 us (8%)
  matrix products  35.4 us (5%)
    all_to_all x11, waiting for transfers between devices, share(): return lax.all_to_all(copies, ALL, 0, 0, tiled=True)  110 us
    all_to_all x5, waiting for transfers between devices, finish_rows(): parts = lax.all_to_all(parts, 'batch', 1, 1, tiled=True)  87.8 us
    all_to_all x4, waiting for transfers between devices, exchange(): return lax.all_to_all(block, 'space', 0, 0, tiled=True)  51 us
    all_to_all x11, starting transfers between devices, share(): return lax.all_to_all(copies, ALL, 0, 0, tiled=True)  38.6 us
    dot_general x21, matrix products, dot(): return lax.dot_general(a, b, (dims, ((), ())), preferred_element_type=F32)  34.9 us
    all_to_all x2, waiting for transfers between devices, finish_cols(): lax.all_to_all(product.reshape(ns, r // ns, c), 'space', 0, 0, tiled=True)  34.2 us
    unnamed x366, local copies, waits for them, and re-layouts  32.2 us
    all_gather x5, blocking collectives, finish_rows(): return lax.all_gather(mine, 'batch', axis=0, tiled=True).astype(F32)  29.2 us
  transfers between devices with their start and end apart: 33, of which 32 were waited for; matrix products, arithmetic and copies ran while one was open for 15% of the time, Pallas kernels for 0%

profile of v1, /device:TPU:0, one launch (start us, length us, event | category | flops | bytes accessed | tf_op | source)
XLA Modules:
  0.0 750.9 jit_solution(12680082690076227233)
XLA Ops:
  9.6 7.3 all-to-all-start.1
  19.3 19.5 %all-to-all-done.1 = f32[32,19,256]{2,1,0:T(8,128)S(1)} async-done(((f32[32,19,256]{2,1,0:T(8,128)}), f32[32,19,256]{2,1,0:T(8,128)S(1)}, u32[]{:S(2)}, u32[]{:S(2)}) %all-to-all-start.1) | async-done | bytes 622624 | tf_op jit(solution)/shard_map/all_to_all | solution.py:32
  43.8 10.2 %all-to-all-done = f32[8,3,16,256]{3,2,1,0:T(8,128)S(1)} async-done(((f32[8,3,16,256]{3,2,1,0:T(8,128)}), f32[8,3,16,256]{3,2,1,0:T(8,128)S(1)}, u32[]{:S(2)}, u32[]{:S(2)}) %all-to-all-start) | async-done | bytes 393248 | tf_op jit(solution)/shard_map/all_to_all | solution.py:139
  63.4 7.4 all-to-all-done.2
  70.9 4.2 all-to-all-start.4
  79.2 16.7 %all-to-all-done.4 = bf16[8,3,16,1024]{3,2,1,0:T(8,128)(2,1)} async-done(((bf16[8,3,16,1024]{3,2,1,0:T(8,128)(2,1)}), bf16[8,3,16,1024]{3,2,1,0:T(8,128)(2,1)}, u32[]{:S(2)}, u32[]{:S(2)}) %all-to-all-start.4) | async-done | bytes 786464 | tf_op jit(solution)/shard_map/all_to_all | solution.py:139
  103.0 19.5 %all-to-all-done.3 = f32[32,3,2,1024]{3,2,1,0:T(2,128)S(1)} async-done(((f32[32,3,2,1024]{3,2,1,0:T(2,128)}), f32[32,3,2,1024]{3,2,1,0:T(2,128)S(1)}, u32[]{:S(2)}, u32[]{:S(2)}) %all-to-all-start.3) | async-done | bytes 786464 | tf_op jit(solution)/shard_map/all_to_all | solution.py:32
  127.6 15.6 %all_to_all.170 = f32[32,3,2,512]{3,2,1,0:T(2,128)S(1)} all-to-all(f32[32,3,2,512]{3,2,1,0:T(2,128)S(1)} %broadcast_in_dim.145), channel_id=1, replica_groups=mesh['batch'=4,'space'=8] {'batch','space'}, dimensions={0} | all-to-all | bytes 786432 | tf_op jit(solution)/shard_map/all_to_all | solution.py:32
  157.2 8.7 %all-to-all-done.6 = f32[32,3,2,512]{3,2,1,0:T(2,128)} async-done(((f32[32,3,2,512]{3,2,1,0:T(2,128)}), f32[32,3,2,512]{3,2,1,0:T(2,128)}, u32[]{:S(2)}, u32[]{:S(2)}) %all-to-all-start.6) | async-done | bytes 393248 | tf_op jit(solution)/shard_map/all_to_all | solution.py:32
  181.2 6.5 all-to-all-done.7
  228.3 5.2 all-to-all-start.9
  234.9 6.0 all-to-all-done.9
  257.9 6.4 all-to-all-done.10
  290.4 13.4 %all-to-all-done.11 = f32[32,3,2,512]{3,2,1,0:T(2,128)S(1)} async-done(((f32[32,3,2,512]{3,2,1,0:T(2,128)}), f32[32,3,2,512]{3,2,1,0:T(2,128)S(1)}, u32[]{:S(2)}, u32[]{:S(2)}) %all-to-all-start.11) | async-done | bytes 393248 | tf_op jit(solution)/shard_map/all_to_all | solution.py:32
  305.5 3.9 fusion.113
  316.9 12.4 %all-to-all-done.12 = f32[32,3,2,512]{3,2,1,0:T(2,128)S(1)} async-done(((f32[32,3,2,512]{3,2,1,0:T(2,128)}), f32[32,3,2,512]{3,2,1,0:T(2,128)S(1)}, u32[]{:S(2)}, u32[]{:S(2)}) %all-to-all-start.12) | async-done | bytes 393248 | tf_op jit(solution)/shard_map/all_to_all | solution.py:32
  330.3 4.2 all-to-all-start.31
  338.7 7.5 all-to-all-done.31
  347.0 4.1 all-to-all-start.28
  351.2 3.8 fusion.28
  362.1 4.1 fusion.135
  383.5 12.4 %all-to-all-done.14 = f32[32,3,2,1024]{3,2,1,0:T(2,128)} async-done(((f32[32,3,2,1024]{3,2,1,0:T(2,128)}), f32[32,3,2,1024]{3,2,1,0:T(2,128)}, u32[]{:S(2)}, u32[]{:S(2)}) %all-to-all-start.14) | async-done | bytes 786464 | tf_op jit(solution)/shard_map/all_to_all | solution.py:32
  415.0 10.0 %all-to-all-done.24 = bf16[8,4,32,512]{3,2,0,1:T(8,128)(2,1)S(1)} async-done(((bf16[8,4,32,512]{3,2,0,1:T(8,128)(2,1)}), bf16[8,4,32,512]{3,2,0,1:T(8,128)(2,1)S(1)}, u32[]{:S(2)}, u32[]{:S(2)}) %all-to-all-start.24) | async-done | bytes 1048608 | tf_op jit(solution)/shard_map/all_to_all | solution.py:291
  433.0 3.9 all-to-all-done.15
  436.9 3.8 all-to-all-start.30
  441.9 13.6 %all-to-all-done.30 = bf16[8,64,512]{2,1,0:T(8,128)(2,1)S(1)} async-done(((bf16[8,64,512]{2,1,0:T(8,128)(2,1)}), bf16[8,64,512]{2,1,0:T(8,128)(2,1)S(1)}, u32[]{:S(2)}, u32[]{:S(2)}) %all-to-all-start.30) | async-done | bytes 524320 | tf_op jit(solution)/shard_map/all_to_all | solution.py:284
  465.1 20.7 %all-to-all-done.33 = bf16[8,128,512]{2,1,0:T(8,128)(2,1)S(1)} async-done(((bf16[8,128,512]{2,1,0:T(8,128)(2,1)}), bf16[8,128,512]{2,1,0:T(8,128)(2,1)S(1)}, u32[]{:S(2)}, u32[]{:S(2)}) %all-to-all-start.33) | async-done | bytes 1048608 | tf_op jit(solution)/shard_map/all_to_all | solution.py:284
  491.2 6.9 all-to-all-done.22
  505.2 5.3 all-to-all-done.25
  516.9 4.5 all-to-all-done.23
  528.2 5.0 all-to-all-done.17
  533.3 3.8 all-to-all-start.16
  544.1 4.8 all-to-all-done.16
  548.9 5.0 all-to-all-start.26
  556.6 51.2 %all-to-all-done.26 = bf16[8,4,144,512]{3,2,0,1:T(8,128)(2,1)} async-done(((bf16[8,4,144,512]{3,2,0,1:T(8,128)(2,1)}), bf16[8,4,144,512]{3,2,0,1:T(8,128)(2,1)}, u32[]{:S(2)}, u32[]{:S(2)}) %all-to-all-start.26) | async-done | bytes 4718624 | tf_op jit(solution)/shard_map/all_to_all | solution.py:291
  615.3 11.9 %all-to-all-done.20 = bf16[8,4,72,256]{3,2,0,1:T(8,128)(2,1)S(1)} async-done(((bf16[8,4,72,256]{3,2,0,1:T(8,128)(2,1)}), bf16[8,4,72,256]{3,2,0,1:T(8,128)(2,1)S(1)}, u32[]{:S(2)}, u32[]{:S(2)}) %all-to-all-start.20) | async-done | bytes 1179680 | tf_op jit(solution)/shard_map/all_to_all | solution.py:291
  631.6 7.9 %all-to-all-done.18 = bf16[8,4,32,256]{3,2,0,1:T(8,128)(2,1)S(1)} async-done(((bf16[8,4,32,256]{3,2,0,1:T(8,128)(2,1)}), bf16[8,4,32,256]{3,2,0,1:T(8,128)(2,1)S(1)}, u32[]{:S(2)}, u32[]{:S(2)}) %all-to-all-start.18) | async-done | bytes 524320 | tf_op jit(solution)/shard_map/all_to_all | solution.py:291
  643.8 19.4 %all-to-all-done.13 = bf16[8,3,16,1024]{3,2,1,0:T(8,128)(2,1)S(1)} async-done(((bf16[8,3,16,1024]{3,2,1,0:T(8,128)(2,1)}), bf16[8,3,16,1024]{3,2,1,0:T(8,128)(2,1)S(1)}, u32[]{:S(2)}, u32[]{:S(2)}) %all-to-all-start.13) | async-done | bytes 786464 | tf_op jit(solution)/shard_map/all_to_all | solution.py:139
  667.7 6.4 all-to-all-done.19
  677.8 4.4 reduce_sum.783
  682.2 4.2 all-to-all-done.21
  695.3 5.8 all_gather.26
  702.7 7.4 all_gather.27
  711.2 5.4 all_gather.24
  718.6 5.2 all_gather.23
  728.5 5.2 all_gather.21
  734.5 5.5 all_gather.22
  740.9 7.8 %all_gather.25 = bf16[576,512]{1,0:T(8,128)(2,1)S(1)} all-gather(bf16[144,512]{1,0:T(8,128)(2,1)S(1)} %reduce_sum.784), channel_id=1, replica_groups=mesh['batch'=4,'space'=8] {'batch'}, dimensions={0}, use_global_device_ids=true | all-gather | bytes 737280 | tf_op jit(solution)/shard_map/all_gather | solution.py:295
  (717 shorter events, 312.5 us)
Async XLA Ops:
  0.7 170.5 %copy-start = (bf16[512,2048]{1,0:T(8,128)(2,1)S(1)}, bf16[512,2048]{1,0:T(8,128)(2,1)}, u32[]{:S(2)}) copy-start(bf16[512,2048]{1,0:T(8,128)(2,1)} %param.31) | copy-start | bytes 6291460
  9.6 29.3 %all-to-all-start.1 = ((f32[32,19,256]{2,1,0:T(8,128)}), f32[32,19,256]{2,1,0:T(8,128)S(1)}, u32[]{:S(2)}, u32[]{:S(2)}) async-start(f32[32,19,256]{2,1,0:T(8,128)} %broadcast_in_dim.141), calls=%async_computation.1 | async-start | bytes 1572864 | tf_op jit(solution)/shard_map/all_to_all | solution.py:32
  19.3 34.7 %copy-start.129 = (f32[256]{0:T(256)S(1)}, f32[256]{0:T(256)}, u32[]{:S(2)}) copy-start(f32[256]{0:T(256)} %param.33) | copy-start | bytes 3076
  19.3 34.7 %copy-start.136 = (f32[256]{0:T(256)S(1)}, f32[256]{0:T(256)}, u32[]{:S(2)}) copy-start(f32[256]{0:T(256)} %param.34) | copy-start | bytes 3076
  38.8 15.2 %all-to-all-start = ((f32[8,3,16,256]{3,2,1,0:T(8,128)}), f32[8,3,16,256]{3,2,1,0:T(8,128)S(1)}, u32[]{:S(2)}, u32[]{:S(2)}) async-start(f32[8,3,16,256]{3,2,1,0:T(8,128)} %get-tuple-element.443), calls=%async_computation | async-start | bytes 786432 | tf_op jit(solution)/shard_map/all_to_all | solution.py:139
  55.0 88.7 %copy-start.118 = (f32[3]{0:T(128)}, f32[3]{0:T(128)S(1)}, u32[]{:S(2)}) copy-start(f32[3]{0:T(128)S(1)} %get-tuple-element.268) | copy-start | bytes 40
  59.0 11.9 %all-to-all-start.2 = ((f32[32,3,2,256]{3,2,1,0:T(2,128)}), f32[32,3,2,256]{3,2,1,0:T(2,128)S(1)}, u32[]{:S(2)}, u32[]{:S(2)}) async-start(f32[32,3,2,256]{3,2,1,0:T(2,128)} %broadcast_in_dim.143), calls=%async_computation.2 | async-start | bytes 393216 | tf_op jit(solution)/shard_map/all_to_all | solution.py:32
  62.8 81.1 %copy-start.110 = (f32[3]{0:T(128)}, f32[3]{0:T(128)S(1)}, u32[]{:S(2)}) copy-start(f32[3]{0:T(128)S(1)} %get-tuple-element.441) | copy-start | bytes 40
  70.9 25.0 %all-to-all-start.4 = ((bf16[8,3,16,1024]{3,2,1,0:T(8,128)(2,1)}), bf16[8,3,16,1024]{3,2,1,0:T(8,128)(2,1)}, u32[]{:S(2)}, u32[]{:S(2)}) async-start(bf16[8,3,16,1024]{3,2,1,0:T(8,128)(2,1)} %bitcast.565.clone.2), calls=%async_computation.4 | async-start | bytes 1572864 | tf_op jit(solution)/shard_map/all_to_all | solution.py:139
  96.9 25.6 %all-to-all-start.3 = ((f32[32,3,2,1024]{3,2,1,0:T(2,128)}), f32[32,3,2,1024]{3,2,1,0:T(2,128)S(1)}, u32[]{:S(2)}, u32[]{:S(2)}) async-start(f32[32,3,2,1024]{3,2,1,0:T(2,128)} %broadcast_in_dim.144), calls=%async_computation.3 | async-start | bytes 1572864 | tf_op jit(solution)/shard_map/all_to_all | solution.py:32
  103.0 20.6 %copy-start.102 = (f32[1024]{0:T(1024)S(1)}, f32[1024]{0:T(1024)}, u32[]{:S(2)}) copy-start(f32[1024]{0:T(1024)} %param.37) | copy-start | bytes 12292
  103.0 21.3 %copy-start.116 = (f32[1024]{0:T(1024)S(1)}, f32[1024]{0:T(1024)}, u32[]{:S(2)}) copy-start(f32[1024]{0:T(1024)} %param.38) | copy-start | bytes 12292
  124.3 22.4 %slice-start = ((s8[4718592]{0:T(1024)(128)(4,1)}), s8[524288]{0:T(1024)(128)(4,1)S(1)}, s32[]{:S(2)}) async-start(s8[4718592]{0:T(1024)(128)(4,1)} %bitcast.670), calls=%async_computation.34 | async-start | bytes 1048576
  127.3 19.4 %slice-start.1 = ((s8[4718592]{0:T(1024)(128)(4,1)}), s8[4194304]{0:T(1024)(128)(4,1)S(1)}, s32[]{:S(2)}) async-start(s8[4718592]{0:T(1024)(128)(4,1)} %bitcast.670), calls=%async_computation.35 | async-start | bytes 8388608
  148.6 17.3 %all-to-all-start.6 = ((f32[32,3,2,512]{3,2,1,0:T(2,128)}), f32[32,3,2,512]{3,2,1,0:T(2,128)}, u32[]{:S(2)}, u32[]{:S(2)}) async-start(f32[32,3,2,512]{3,2,1,0:T(2,128)} %broadcast_in_dim.146), calls=%async_computation.6 | async-start | bytes 786432 | tf_op jit(solution)/shard_map/all_to_all | solution.py:32
  176.7 11.0 %all-to-all-start.7 = ((f32[32,6,128]{2,1,0:T(8,128)}), f32[32,6,128]{2,1,0:T(8,128)}, u32[]{:S(2)}, u32[]{:S(2)}) async-start(f32[32,6,128]{2,1,0:T(8,128)} %copy.563), calls=%async_computation.7 | async-start | bytes 262144 | tf_op jit(solution)/shard_map/all_to_all | solution.py:36
  196.2 11.8 %all-to-all-start.8 = ((f32[32,3,2,2,128]{4,3,2,1,0:T(2,128)}), f32[32,3,2,2,128]{4,3,2,1,0:T(2,128)}, u32[]{:S(2)}, u32[]{:S(2)}) async-start(f32[32,3,2,2,128]{4,3,2,1,0:T(2,128)} %broadcast_in_dim.148), calls=%async_computation.8 | async-start | bytes 393216 | tf_op jit(solution)/shard_map/all_to_all | solution.py:32
  228.3 12.7 %all-to-all-start.9 = ((f32[32,1,576]{2,1,0:T(1,128)}), f32[32,1,576]{2,1,0:T(1,128)}, u32[]{:S(2)}, u32[]{:S(2)}) async-start(f32[32,1,576]{2,1,0:T(1,128)} %reshape.1076), calls=%async_computation.9 | async-start | bytes 163840 | tf_op jit(solution)/shard_map/all_to_all | solution.py:36
  253.3 11.1 %all-to-all-start.10 = ((f32[32,1,1152]{2,1,0:T(1,128)}), f32[32,1,1152]{2,1,0:T(1,128)}, u32[]{:S(2)}, u32[]{:S(2)}) async-start(f32[32,1,1152]{2,1,0:T(1,128)} %reshape.1078), calls=%async_computation.10 | async-start | bytes 294912 | tf_op jit(solution)/shard_map/all_to_all | solution.py:32
  287.5 16.3 %all-to-all-start.11 = ((f32[32,3,2,512]{3,2,1,0:T(2,128)}), f32[32,3,2,512]{3,2,1,0:T(2,128)S(1)}, u32[]{:S(2)}, u32[]{:S(2)}) async-start(f32[32,3,2,512]{3,2,1,0:T(2,128)} %broadcast_in_dim.151), calls=%async_computation.11 | async-start | bytes 786432 | tf_op jit(solution)/shard_map/all_to_all | solution.py:32
  313.1 16.1 %all-to-all-start.12 = ((f32[32,3,2,512]{3,2,1,0:T(2,128)}), f32[32,3,2,512]{3,2,1,0:T(2,128)S(1)}, u32[]{:S(2)}, u32[]{:S(2)}) async-start(f32[32,3,2,512]{3,2,1,0:T(2,128)} %broadcast_in_dim.152), calls=%async_computation.12 | async-start | bytes 786432 | tf_op jit(solution)/shard_map/all_to_all | solution.py:32
  330.3 15.9 %all-to-all-start.31 = ((bf16[4,96,1024]{2,1,0:T(8,128)(2,1)}), bf16[4,96,1024]{2,1,0:T(8,128)(2,1)}, u32[]{:S(2)}, u32[]{:S(2)}) async-start(bf16[4,96,1024]{2,1,0:T(8,128)(2,1)} %broadcast_in_dim.185), calls=%async_computation.31 | async-start | bytes 1572864 | tf_op jit(solution)/shard_map/all_to_all | solution.py:279
  347.0 11.6 %all-to-all-start.28 = ((bf16[4,96,512]{2,1,0:T(8,128)(2,1)}), bf16[4,96,512]{2,1,0:T(8,128)(2,1)}, u32[]{:S(2)}, u32[]{:S(2)}) async-start(bf16[4,96,512]{2,1,0:T(8,128)(2,1)} %broadcast_in_dim.183), calls=%async_computation.28 | async-start | bytes 786432 | tf_op jit(solution)/shard_map/all_to_all | solution.py:279
  358.6 10.9 %all-to-all-start.32 = ((bf16[4,96,512]{2,1,0:T(8,128)(2,1)}), bf16[4,96,512]{2,1,0:T(8,128)(2,1)S(1)}, u32[]{:S(2)}, u32[]{:S(2)}) async-start(bf16[4,96,512]{2,1,0:T(8,128)(2,1)} %bitcast.697), calls=%async_computation.32 | async-start | bytes 786432 | tf_op jit(solution)/shard_map/all_to_all | solution.py:277
  370.6 25.3 %all-to-all-start.14 = ((f32[32,3,2,1024]{3,2,1,0:T(2,128)}), f32[32,3,2,1024]{3,2,1,0:T(2,128)}, u32[]{:S(2)}, u32[]{:S(2)}) async-start(f32[32,3,2,1024]{3,2,1,0:T(2,128)} %broadcast_in_dim.158), calls=%async_computation.14 | async-start | bytes 1572864 | tf_op jit(solution)/shard_map/all_to_all | solution.py:32
  380.4 19.0 %copy-start.8 = (bf16[3,128,1024]{2,1,0:T(8,128)(2,1)S(1)}, bf16[3,128,1024]{2,1,0:T(8,128)(2,1)}, u32[]{:S(2)}) copy-start(bf16[3,128,1024]{2,1,0:T(8,128)(2,1)} %copy-done.7) | copy-start | bytes 2359300
  380.4 19.0 %copy-start.30 = (bf16[3,128,512]{2,1,0:T(8,128)(2,1)S(1)}, bf16[3,128,512]{2,1,0:T(8,128)(2,1)}, u32[]{:S(2)}) copy-start(bf16[3,128,512]{2,1,0:T(8,128)(2,1)} %copy-done.29) | copy-start | bytes 1179652
  395.9 10.9 %all-to-all-start.29 = ((bf16[4,96,512]{2,1,0:T(8,128)(2,1)}), bf16[4,96,512]{2,1,0:T(8,128)(2,1)S(1)}, u32[]{:S(2)}, u32[]{:S(2)}) async-start(bf16[4,96,512]{2,1,0:T(8,128)(2,1)} %bitcast.634), calls=%async_computation.29 | async-start | bytes 786432 | tf_op jit(solution)/shard_map/all_to_all | solution.py:277
  406.8 18.1 %all-to-all-start.24 = ((bf16[8,4,32,512]{3,2,0,1:T(8,128)(2,1)}), bf16[8,4,32,512]{3,2,0,1:T(8,128)(2,1)S(1)}, u32[]{:S(2)}, u32[]{:S(2)}) async-start(bf16[8,4,32,512]{3,2,0,1:T(8,128)(2,1)} %copy.612), calls=%async_computation.24 | async-start | bytes 2097152 | tf_op jit(solution)/shard_map/all_to_all | solution.py:291
  425.7 11.3 %all-to-all-start.15 = ((f32[32,3,2,256]{3,2,1,0:T(2,128)}), f32[32,3,2,256]{3,2,1,0:T(2,128)S(1)}, u32[]{:S(2)}, u32[]{:S(2)}) async-start(f32[32,3,2,256]{3,2,1,0:T(2,128)} %broadcast_in_dim.159), calls=%async_computation.15 | async-start | bytes 393216 | tf_op jit(solution)/shard_map/all_to_all | solution.py:32
  436.9 18.5 %all-to-all-start.30 = ((bf16[8,64,512]{2,1,0:T(8,128)(2,1)}), bf16[8,64,512]{2,1,0:T(8,128)(2,1)S(1)}, u32[]{:S(2)}, u32[]{:S(2)}) async-start(bf16[8,64,512]{2,1,0:T(8,128)(2,1)} %bitcast.158), calls=%async_computation.30 | async-start | bytes 1048576 | tf_op jit(solution)/shard_map/all_to_all | solution.py:284
  441.6 20.9 %copy-start.23 = (bf16[3,128,256]{2,1,0:T(8,128)(2,1)}, bf16[3,128,256]{2,1,0:T(8,128)(2,1)S(1)}, u32[]{:S(2)}) copy-start(bf16[3,128,256]{2,1,0:T(8,128)(2,1)S(1)} %multiply_convert_fusion.8) | copy-start | bytes 589828
  456.3 29.6 %all-to-all-start.33 = ((bf16[8,128,512]{2,1,0:T(8,128)(2,1)}), bf16[8,128,512]{2,1,0:T(8,128)(2,1)S(1)}, u32[]{:S(2)}, u32[]{:S(2)}) async-start(bf16[8,128,512]{2,1,0:T(8,128)(2,1)} %bitcast.162), calls=%async_computation.33 | async-start | bytes 2097152 | tf_op jit(solution)/shard_map/all_to_all | solution.py:284
  463.1 26.8 %copy-start.48 = (bf16[3,4,8,2304]{3,2,1,0:T(8,128)(2,1)}, bf16[3,4,8,2304]{3,2,1,0:T(8,128)(2,1)S(1)}, u32[]{:S(2)}) copy-start(bf16[3,4,8,2304]{3,2,1,0:T(8,128)(2,1)S(1)} %get-tuple-element.315) | copy-start | bytes 1327108
  463.8 26.1 %copy-start.49 = (bf16[3,4,8,2304]{3,2,1,0:T(8,128)(2,1)}, bf16[3,4,8,2304]{3,2,1,0:T(8,128)(2,1)S(1)}, u32[]{:S(2)}) copy-start(bf16[3,4,8,2304]{3,2,1,0:T(8,128)(2,1)S(1)} %get-tuple-element.356) | copy-start | bytes 1327108
  485.8 12.3 %all-to-all-start.22 = ((bf16[8,4,8,1024]{3,2,0,1:T(8,128)(2,1)}), bf16[8,4,8,1024]{3,2,0,1:T(8,128)(2,1)S(1)}, u32[]{:S(2)}, u32[]{:S(2)}) async-start(bf16[8,4,8,1024]{3,2,0,1:T(8,128)(2,1)} %copy.610), calls=%async_computation.22 | async-start | bytes 1048576 | tf_op jit(solution)/shard_map/all_to_all | solution.py:291
  498.1 12.4 %all-to-all-start.25 = ((bf16[8,32,512]{2,1,0:T(8,128)(2,1)}), bf16[8,32,512]{2,1,0:T(8,128)(2,1)S(1)}, u32[]{:S(2)}, u32[]{:S(2)}) async-start(bf16[8,32,512]{2,1,0:T(8,128)(2,1)} %reduce_sum.781), calls=%async_computation.25 | async-start | bytes 524288 | tf_op jit(solution)/shard_map/all_to_all | solution.py:293
  510.5 10.9 %all-to-all-start.23 = ((bf16[8,8,1024]{2,1,0:T(8,128)(2,1)}), bf16[8,8,1024]{2,1,0:T(8,128)(2,1)S(1)}, u32[]{:S(2)}, u32[]{:S(2)}) async-start(bf16[8,8,1024]{2,1,0:T(8,128)(2,1)} %reduce_sum.779), calls=%async_computation.23 | async-start | bytes 262144 | tf_op jit(solution)/shard_map/all_to_all | solution.py:293
  522.1 11.1 %all-to-all-start.17 = ((f32[32,3,2,256]{3,2,1,0:T(2,128)}), f32[32,3,2,256]{3,2,1,0:T(2,128)S(1)}, u32[]{:S(2)}, u32[]{:S(2)}) async-start(f32[32,3,2,256]{3,2,1,0:T(2,128)} %broadcast_in_dim.160), calls=%async_computation.17 | async-start | bytes 393216 | tf_op jit(solution)/shard_map/all_to_all | solution.py:32
  533.3 15.6 %all-to-all-start.16 = ((f32[8,3,16,256]{3,2,1,0:T(8,128)}), f32[8,3,16,256]{3,2,1,0:T(8,128)S(1)}, u32[]{:S(2)}, u32[]{:S(2)}) async-start(f32[8,3,16,256]{3,2,1,0:T(8,128)} %bitcast.125), calls=%async_computation.16 | async-start | bytes 786432 | tf_op jit(solution)/shard_map/all_to_all | solution.py:139
  548.9 58.9 %all-to-all-start.26 = ((bf16[8,4,144,512]{3,2,0,1:T(8,128)(2,1)}), bf16[8,4,144,512]{3,2,0,1:T(8,128)(2,1)}, u32[]{:S(2)}, u32[]{:S(2)}) async-start(bf16[8,4,144,512]{3,2,0,1:T(8,128)(2,1)} %copy.613), calls=%async_computation.26 | async-start | bytes 9437184 | tf_op jit(solution)/shard_map/all_to_all | solution.py:291
  607.8 19.4 %all-to-all-start.20 = ((bf16[8,4,72,256]{3,2,0,1:T(8,128)(2,1)}), bf16[8,4,72,256]{3,2,0,1:T(8,128)(2,1)S(1)}, u32[]{:S(2)}, u32[]{:S(2)}) async-start(bf16[8,4,72,256]{3,2,0,1:T(8,128)(2,1)} %copy.608), calls=%async_computation.20 | async-start | bytes 2359296 | tf_op jit(solution)/shard_map/all_to_all | solution.py:291
  627.2 12.3 %all-to-all-start.18 = ((bf16[8,4,32,256]{3,2,0,1:T(8,128)(2,1)}), bf16[8,4,32,256]{3,2,0,1:T(8,128)(2,1)S(1)}, u32[]{:S(2)}, u32[]{:S(2)}) async-start(bf16[8,4,32,256]{3,2,0,1:T(8,128)(2,1)} %copy.607), calls=%async_computation.18 | async-start | bytes 1048576 | tf_op jit(solution)/shard_map/all_to_all | solution.py:291
  639.5 23.8 %all-to-all-start.13 = ((bf16[8,3,16,1024]{3,2,1,0:T(8,128)(2,1)}), bf16[8,3,16,1024]{3,2,1,0:T(8,128)(2,1)S(1)}, u32[]{:S(2)}, u32[]{:S(2)}) async-start(bf16[8,3,16,1024]{3,2,1,0:T(8,128)(2,1)} %bitcast.103), calls=%async_computation.13 | async-start | bytes 1572864 | tf_op jit(solution)/shard_map/all_to_all | solution.py:139
  663.2 10.8 %all-to-all-start.19 = ((bf16[8,32,256]{2,1,0:T(8,128)(2,1)}), bf16[8,32,256]{2,1,0:T(8,128)(2,1)S(1)}, u32[]{:S(2)}, u32[]{:S(2)}) async-start(bf16[8,32,256]{2,1,0:T(8,128)(2,1)} %reduce_sum.775), calls=%async_computation.19 | async-start | bytes 262144 | tf_op jit(solution)/shard_map/all_to_all | solution.py:293
  674.1 12.3 %all-to-all-start.21 = ((bf16[8,72,256]{2,1,0:T(8,128)(2,1)}), bf16[8,72,256]{2,1,0:T(8,128)(2,1)S(1)}, u32[]{:S(2)}, u32[]{:S(2)}) async-start(bf16[8,72,256]{2,1,0:T(8,128)(2,1)} %reduce_sum.777), calls=%async_computation.21 | async-start | bytes 589824 | tf_op jit(solution)/shard_map/all_to_all | solution.py:293
  687.1 53.6 %all-to-all-start.27 = ((bf16[8,144,512]{2,1,0:T(8,128)(2,1)}), bf16[8,144,512]{2,1,0:T(8,128)(2,1)S(1)}, u32[]{:S(2)}, u32[]{:S(2)}) async-start(bf16[8,144,512]{2,1,0:T(8,128)(2,1)} %reduce_sum.783), calls=%async_computation.27 | async-start | bytes 2359296 | tf_op jit(solution)/shard_map/all_to_all | solution.py:293
  692.9 57.0 %copy-start.107 = (f32[2048]{0:T(1024)}, f32[2048]{0:T(1024)S(1)}, u32[]{:S(2)}) copy-start(f32[2048]{0:T(1024)S(1)} %squeeze.280) | copy-start | bytes 24580
  (127 other events, 939.8 us)
